TPU v7x, 32 devices: a whole 2x2x4 slice. The times are simulated.
32 devices in a mesh: sub: 16 (over z, y, x), coarse: 2 (over core).
Axes of the slice: x: 2, y: 2, z: 4, core: 2. Of those that a mesh axis runs over, the one named last changes fastest.
Arguments:
- right_side: float32 [16, 64, 256], P('sub', None, 'coarse'), may hold values from -6 to 6
- local_blocks: bfloat16 [16, 2, 64, 64, 256], P('sub', None, None, None, 'coarse'), may hold values from -0.5 to 0.5
- diag_blocks: bfloat16 [16, 64, 64, 256], P('sub', None, None, 'coarse'), as said below
- iface_blocks: bfloat16 [16, 64, 64, 192], P('sub', None, None, 'coarse'), may hold values from -0.75 to 0.75
- block_cols: int32 [16, 2, 256], P('sub', None, 'coarse'), may hold values from 0 to 255
- basis: bfloat16 [16, 32, 64, 256], P('sub', None, None, 'coarse'), may hold values from -0.09375 to 0.09375
- coarse_inverse: float32 [512, 512], P('sub'), as said below
Outputs:
- solution_field: float32 [16, 64, 256], P('sub', None, 'coarse')
- residual: float32 [16, 64, 256], P('sub', None, 'coarse')
Inputs may be any that keep to these rules, and one draw needn't show every extreme that they name: `diag_blocks`: each diagonal block is 4 times the identity plus entries of magnitude at most 0.5. `coarse_inverse`: the matrix is the identity plus entries of magnitude at most 4 / sqrt(512).
All inputs are finite; a program needn't handle non-finite values.
Results may differ from a plain program's by a relative error of at most 0.0003.
Values sent between devices are 32-bit elements; how exact they have to be, the bound alone decides.
No kernel may reach another device: no remote copies, remote signals or barrier semaphores. Data moves between devices by JAX's collectives and lax.ppermute only.
A program may use at most 64 MiB of HBM per device.

v0:
```python
import functools

import jax
import jax.numpy as jnp
from jax import lax
from jax.experimental import pallas as pl
from jax.experimental.pallas import tpu as pltpu
from jax.sharding import PartitionSpec as P

SWEEPS = 3
ITERS = 2
ROWS = 8
HIGH = lax.Precision.HIGHEST


def in_vmem(array):
    return pltpu.with_memory_space_constraint(array, pltpu.VMEM)


def call(body, outs, *args, macs=0):
    args = [in_vmem(a) for a in args]
    size = sum(a.size * a.dtype.itemsize for a in args)
    return pl.pallas_call(
        body,
        out_shape=[pltpu.VMEM(shape, jnp.float32) for shape in outs],
        in_specs=[pl.BlockSpec(memory_space=pltpu.VMEM) for _ in args],
        out_specs=[pl.BlockSpec(memory_space=pltpu.VMEM) for _ in outs],
        cost_estimate=pl.CostEstimate(flops=2 * macs, bytes_accessed=size, transcendentals=0),
    )(*args)


def rows_times(blocks, vec, start):
    chunk = blocks[pl.ds(start, ROWS)].astype(jnp.float32)
    return jnp.sum(chunk * vec[None], axis=1)


def by_rows(count, body):
    def step(at, carry):
        body(pl.multiple_of(at * ROWS, ROWS))
        return carry

    lax.fori_loop(0, count // ROWS, step, 0)


def block_product(blocks, vec, out):
    def body(start):
        out[pl.ds(start, ROWS), :] = rows_times(blocks, vec, start)

    by_rows(blocks.shape[0], body)


def relaxed(dblock, vec, out, base=None):
    def body(start):
        part = dblock_rows(dblock, vec, start)
        value = part if base is None else base[pl.ds(start, ROWS), :] + part
        out[pl.ds(start, ROWS), :] = value

    whole = vec[...]

    def dblock_rows(blocks, ref, start):
        return 0.25 * (2.0 * ref[pl.ds(start, ROWS), :] - 0.25 * rows_times(blocks, whole, start))

    by_rows(dblock.shape[0], body)


def restricted(zvec, vec, scratch, sub):
    block_product(zvec, vec, scratch)
    nvec = scratch.shape[0]
    lanes = scratch.shape[1]
    copies = lanes // nvec
    part = scratch[...]
    stacked = jnp.concatenate([part] * copies, axis=0)
    ones = jnp.ones((8, lanes), jnp.float32)
    sums = lax.dot_general(
        ones, stacked, (((1,), (1,)), ((), ())), precision=HIGH, preferred_element_type=jnp.float32
    )
    lane = lax.broadcasted_iota(jnp.int32, sums.shape, 1)
    row = lax.broadcasted_iota(jnp.int32, sums.shape, 0)
    keep = (lane // nvec == lax.rem(sub, copies)) & (row == 0)
    return jnp.where(keep, sums, 0.0)


def spread(message, cross, square):
    row = lax.broadcasted_iota(jnp.int32, message.shape, 0)
    return jnp.where(row == 1, cross, jnp.where(row == 2, square, message))


def total(x):
    return jnp.sum(x, keepdims=True)


def first_kernel(resid, dblock, zvec, state, message, scratch):
    relaxed(dblock, resid, state)
    message[...] = jnp.broadcast_to(
        restricted(zvec, resid[...], scratch, lax.axis_index("sub"))[None], message.shape
    )


def diag_kernel(vec, dblock, out):
    block_product(dblock, vec[...], out)


def picked(vec, others, cols, part):
    me = lax.axis_index("coarse")
    width = vec.shape[1]
    index = jnp.broadcast_to(cols[pl.ds(part, 1), :], vec.shape)
    owner = index // width
    place = lax.rem(index, width)

    def lanes(block):
        return jnp.take_along_axis(block, place, axis=1, mode="promise_in_bounds")

    if others.shape[0] == 1:
        return jnp.where(owner == me, lanes(vec[...]), lanes(others[0]))
    value = lanes(others[0])
    for at in range(1, others.shape[0]):
        value = jnp.where(owner == at, lanes(others[at]), value)
    return value


def off_rows(lblocks, chosen, start):
    value = rows_times(lblocks.at[0], chosen[0], start)
    for part in range(1, len(chosen)):
        value = value + rows_times(lblocks.at[part], chosen[part], start)
    return value


def sweep_kernel(state, others, own, resid, dblock, lblocks, cols, out, rest):
    chosen = [picked(state, others, cols, part) for part in range(lblocks.shape[0])]

    def body(start):
        here = pl.ds(start, ROWS)
        rest[here, :] = resid[here, :] - (own[here, :] + off_rows(lblocks, chosen, start))

    by_rows(dblock.shape[0], body)
    relaxed(dblock, rest, out, state)


def off_kernel(vec, others, own, lblocks, cols, out):
    chosen = [picked(vec, others, cols, part) for part in range(lblocks.shape[0])]

    def body(start):
        out[pl.ds(start, ROWS), :] = own[pl.ds(start, ROWS), :] + off_rows(lblocks, chosen, start)

    by_rows(out.shape[0], body)


def step_size(arrived):
    cross = jnp.sum(arrived[:, 1, :], axis=0, keepdims=True)
    square = jnp.sum(arrived[:, 2, :], axis=0, keepdims=True)
    return cross / (square + 1e-06)


def corrected(state, arrived, inverse, zvec, count):
    nvec = zvec.shape[0]
    lanes = state.shape[1]
    each = count * (lanes // nvec)
    acc = jnp.zeros((nvec, lanes), jnp.float32)
    for at in range(inverse.shape[1] // lanes):
        row = jnp.sum(arrived[at * each : (at + 1) * each, 0, :], axis=0, keepdims=True)
        acc = acc + inverse[:, at * lanes : (at + 1) * lanes] * row
    weights = jnp.broadcast_to(jnp.sum(acc, axis=1, keepdims=True), acc.shape)
    value = state[...]
    for at in range(nvec):
        value = value + weights[at : at + 1, :] * zvec[at].astype(jnp.float32)
    return value


def direction_kernel(count, state, arrived, inverse, zvec, out):
    out[...] = corrected(state, arrived, inverse, zvec, count)


def next_direction_kernel(count, state, arrived, inverse, zvec, previous, resid, image, out, rest, alpha):
    size = step_size(arrived)
    out[...] = previous[...] - size * corrected(state, arrived, inverse, zvec, count)
    rest[...] = resid[...] - size * image[...]
    alpha[...] = jnp.broadcast_to(size, alpha.shape)


def near(parts, inner):
    lane = lax.broadcasted_iota(jnp.int32, parts[0].shape, 1)
    value = parts[0][...]
    for at in range(1, len(parts)):
        value = jnp.where(lane < at * inner, value, parts[at][...])
    return value[:, : len(parts) * inner]


def with_interface(known, parts, fblock, out):
    width = fblock.shape[2]
    vec = near(parts, width // len(parts))

    def body(start):
        here = pl.ds(start, ROWS)
        add = rows_times(fblock, vec, start)
        pad = jnp.zeros((ROWS, out.shape[1] - width), jnp.float32)
        out[here, :] = known[here, :] + jnp.concatenate([add, pad], axis=1)

    by_rows(out.shape[0], body)


def image_kernel(known, near0, near1, near2, fblock, resid, dblock, zvec, image, state, message, scratch):
    with_interface(known, (near0, near1, near2), fblock, image)
    relaxed(dblock, image, state)
    value = image[...]
    row = restricted(zvec, value, scratch, lax.axis_index("sub"))
    row = spread(row, total(resid[...] * value), total(value * value))
    message[...] = jnp.broadcast_to(row[None], message.shape)


def last_image_kernel(known, near0, near1, near2, fblock, resid, image, message):
    with_interface(known, (near0, near1, near2), fblock, image)
    value = image[...]
    row = spread(jnp.zeros(message.shape[1:], jnp.float32), total(resid[...] * value), total(value * value))
    message[...] = jnp.broadcast_to(row[None], message.shape)


def final_kernel(arrived, alpha, first, second, resid, image, field, rest):
    size = step_size(arrived)
    field[...] = alpha[0:1, :] * first[...] + size * second[...]
    rest[...] = resid[...] - size * image[...]


def swap(count, apart):
    return [(low, low ^ apart) for low in range(count) if low ^ apart < count]


def gathered(vec, count):
    if count == 2:
        return lax.ppermute(vec, "coarse", swap(2, 1))[None]
    return lax.all_gather(vec, "coarse", axis=0)


def local(subs, count, right_side, local_blocks, diag_blocks, iface_blocks, block_cols, basis, coarse_inverse):
    lblocks, dblock, fblock = local_blocks[0], diag_blocks[0], iface_blocks[0]
    cols, zvec, resid = block_cols[0], basis[0], right_side[0]
    shape = resid.shape
    devices = subs * count
    parcel = (devices, 8, shape[1])
    scratch = (zvec.shape[0], shape[1])
    lblocks, dblock, fblock, zvec, inverse = map(in_vmem, (lblocks, dblock, fblock, zvec, coarse_inverse))
    resid, cols = in_vmem(resid), in_vmem(cols)

    def everywhere(message):
        return lax.all_to_all(message, ("sub", "coarse"), 0, 0)

    def smooth(resid, state):
        for sweep in range(SWEEPS - 1):
            others = gathered(state, count)
            (own,) = call(diag_kernel, [shape], state, dblock, macs=dblock.size)
            state, _ = call(
                sweep_kernel, [shape, shape], state, others, own, resid, dblock, lblocks, cols,
                macs=dblock.size + lblocks.size,
            )
        return state

    def apply(vec):
        others = gathered(vec, count)
        near_parts = [lax.ppermute(vec, "sub", swap(subs, 1 << bit)) for bit in range(3)]
        (own,) = call(diag_kernel, [shape], vec, dblock, macs=dblock.size)
        (known,) = call(off_kernel, [shape], vec, others, own, lblocks, cols, macs=lblocks.size)
        return [known, *near_parts, fblock]

    state, message, _ = call(
        first_kernel, [shape, parcel, scratch], resid, dblock, zvec, macs=dblock.size + zvec.size
    )
    arrived = everywhere(message)
    state = smooth(resid, state)
    (first,) = call(
        functools.partial(direction_kernel, count), [shape], state, arrived, inverse, zvec, macs=zvec.size
    )
    image, state, message, _ = call(
        image_kernel, [shape, shape, parcel, scratch], *apply(first), resid, dblock, zvec,
        macs=dblock.size + zvec.size + fblock.size,
    )
    arrived = everywhere(message)
    state = smooth(image, state)
    second, rest, alpha = call(
        functools.partial(next_direction_kernel, count), [shape, shape, (8, shape[1])],
        state, arrived, inverse, zvec, first, resid, image, macs=zvec.size,
    )
    image, message = call(last_image_kernel, [shape, parcel], *apply(second), rest, macs=fblock.size)
    arrived = everywhere(message)
    field, rest = call(final_kernel, [shape, shape], arrived, alpha, first, second, rest, image)
    return field[None], rest[None]


def solution(mesh):
    placed = (
        P("sub", None, "coarse"),
        P("sub", None, None, None, "coarse"),
        P("sub", None, None, "coarse"),
        P("sub", None, None, "coarse"),
        P("sub", None, "coarse"),
        P("sub", None, None, "coarse"),
        P("sub", None),
    )
    return jax.shard_map(
        functools.partial(local, mesh.shape["sub"], mesh.shape["coarse"]),
        mesh=mesh,
        in_specs=placed,
        out_specs=(P("sub", None, "coarse"), P("sub", None, "coarse")),
        check_vma=False,
    )
```

profile of v0, /device:TPU:0, one launch (start us, length us, event | category | flops | bytes accessed | tf_op | source)
XLA Modules:
  0.0 89.7 jit_solution(17673966776457776795)
XLA Ops:
  0.7 1.2 %copy-done = bf16[1,64,64,128]{3,2,1,0:T(8,128)(2,1)S(1)} copy-done((bf16[1,64,64,128]{3,2,1,0:T(8,128)(2,1)S(1)}, bf16[1,64,64,128]{3,2,1,0:T(8,128)(2,1)}, u32[]{:S(2)}) %copy-start) | copy-done | bytes 1048600
  1.9 1.0 %copy-done.15 = bf16[1,32,64,128]{3,2,1,0:T(8,128)(2,1)S(1)} copy-done((bf16[1,32,64,128]{3,2,1,0:T(8,128)(2,1)S(1)}, bf16[1,32,64,128]{3,2,1,0:T(8,128)(2,1)}, u32[]{:S(2)}) %copy-start.15) | copy-done | bytes 524312
  2.9 0.8 copy-done.21
  3.7 1.4 %shard_map.86 = (f32[64,128]{1,0:T(8,128)S(1)}, f32[32,8,128]{2,1,0:T(8,128)}, f32[32,128]{1,0:T(8,128)}) custom-call(f32[64,128]{1,0:T(8,128)S(1)} %bitcast.40, bf16[64,64,128]{2,1,0:T(8,128)(2,1)S(1)} %bitcast.16, bf16[32,64,128]{2,1,0:T(8,128)(2,1)S(1)} %bitcast.34), custom_call_target="tpu_custom_call" | custom-call | flops 1572864 | bytes 1605632 | tf_op jit(solution)/shard_map/pallas_call | solution.py:23
  5.0 7.3 %all-to-all-start = ((f32[32,8,128]{2,1,0:T(8,128)}), f32[32,8,128]{2,1,0:T(8,128)S(1)}, u32[]{:S(2)}, u32[]{:S(2)}) async-start(f32[32,8,128]{2,1,0:T(8,128)} %get-tuple-element.21), calls=%async_computation | async-start | bytes 262144 | tf_op jit(solution)/shard_map/all_to_all | solution.py:244
  13.6 1.2 %copy-done.2 = bf16[1,64,64,128]{3,2,1,0:T(8,128)(2,1)S(1)} copy-done((bf16[1,64,64,128]{3,2,1,0:T(8,128)(2,1)S(1)}, bf16[1,64,64,128]{3,2,1,0:T(8,128)(2,1)}, u32[]{:S(2)}) %copy-start.2) | copy-done | bytes 1048600
  14.8 1.6 %copy-done.9 = bf16[1,2,64,64,128]{4,3,2,1,0:T(8,128)(2,1)S(1)} copy-done((bf16[1,2,64,64,128]{4,3,2,1,0:T(8,128)(2,1)S(1)}, bf16[1,2,64,64,128]{4,3,2,1,0:T(8,128)(2,1)}, u32[]{:S(2)}) %copy-start.9) | copy-done | bytes 2097176
  16.4 1.6 %shard_map.88 = (f32[64,128]{1,0:T(8,128)S(1)}, f32[64,128]{1,0:T(8,128)}) custom-call(f32[64,128]{1,0:T(8,128)S(1)} %get-tuple-element.18.vec.state, f32[1,64,128]{2,1,0:T(8,128)S(1)} %bitcast.54, f32[64,128]{1,0:T(8,128)S(1)} %shard_map.87.own, f32[64,128]{1,0:T(8,128)S(1)} %bitcast.41, bf16[64,64,128]{2,1,0:T(8,128)(2,1)S(1)} %bitcast.18, ...), custom_call_target="tpu_custom_call" | custom-call | flops 3145728 | bytes 3277824 | tf_op jit(solution)/shard_map/pallas_call | solution.py:23
  18.3 1.2 %copy-done.3 = bf16[1,64,64,128]{3,2,1,0:T(8,128)(2,1)S(1)} copy-done((bf16[1,64,64,128]{3,2,1,0:T(8,128)(2,1)S(1)}, bf16[1,64,64,128]{3,2,1,0:T(8,128)(2,1)}, u32[]{:S(2)}) %copy-start.3) | copy-done | bytes 1048600
  19.9 1.2 %copy-done.4 = bf16[1,64,64,128]{3,2,1,0:T(8,128)(2,1)S(1)} copy-done((bf16[1,64,64,128]{3,2,1,0:T(8,128)(2,1)S(1)}, bf16[1,64,64,128]{3,2,1,0:T(8,128)(2,1)}, u32[]{:S(2)}) %copy-start.4) | copy-done | bytes 1048600
  21.1 1.6 %copy-done.10 = bf16[1,2,64,64,128]{4,3,2,1,0:T(8,128)(2,1)S(1)} copy-done((bf16[1,2,64,64,128]{4,3,2,1,0:T(8,128)(2,1)S(1)}, bf16[1,2,64,64,128]{4,3,2,1,0:T(8,128)(2,1)}, u32[]{:S(2)}) %copy-start.10) | copy-done | bytes 2097176
  22.7 0.8 copy-done.34
  23.4 1.6 %shard_map.90 = (f32[64,128]{1,0:T(8,128)S(1)}, f32[64,128]{1,0:T(8,128)}) custom-call(f32[64,128]{1,0:T(8,128)S(1)} %copy-done.34, f32[1,64,128]{2,1,0:T(8,128)S(1)} %bitcast.55, f32[64,128]{1,0:T(8,128)S(1)} %shard_map.89.own, f32[64,128]{1,0:T(8,128)S(1)} %bitcast.42, bf16[64,64,128]{2,1,0:T(8,128)(2,1)S(1)} %bitcast.20, ...), custom_call_target="tpu_custom_call" | custom-call | flops 3145728 | bytes 3277824 | tf_op jit(solution)/shard_map/pallas_call | solution.py:23
  26.3 1.0 %copy-done.16 = bf16[1,32,64,128]{3,2,1,0:T(8,128)(2,1)S(1)} copy-done((bf16[1,32,64,128]{3,2,1,0:T(8,128)(2,1)S(1)}, bf16[1,32,64,128]{3,2,1,0:T(8,128)(2,1)}, u32[]{:S(2)}) %copy-start.16) | copy-done | bytes 524312
  27.3 0.9 %copy-done.26 = f32[32,8,128]{2,1,0:T(8,128)S(1)} copy-done((f32[32,8,128]{2,1,0:T(8,128)S(1)}, f32[32,8,128]{2,1,0:T(8,128)}, u32[]{:S(2)}) %copy-start.26) | copy-done | bytes 131096
  28.2 0.8 copy-done.29
  29.1 0.8 copy-done.50
  30.4 1.8 %collective-permute-start.5 = (f32[64,128]{1,0:T(8,128)S(1)}, f32[64,128]{1,0:T(8,128)S(1)}, u32[]{:S(2)}, u32[]{:S(2)}) collective-permute-start(f32[64,128]{1,0:T(8,128)S(1)} %shard_map.91.vec.previous.first), channel_id=1, source_target_pairs={{0,8},{2,10},{4,12},{6,14},{8,0},{10,2},{12,4},{14,6},{16,24},{18,... | collective-permute-start | bytes 98312 | tf_op jit(solution)/shard_map/ppermute | solution.py:258
  32.2 1.5 %collective-permute-start.4 = (f32[64,128]{1,0:T(8,128)S(1)}, f32[64,128]{1,0:T(8,128)S(1)}, u32[]{:S(2)}, u32[]{:S(2)}) collective-permute-start(f32[64,128]{1,0:T(8,128)S(1)} %shard_map.91.vec.previous.first), channel_id=1, source_target_pairs={{0,4},{2,6},{4,0},{6,2},{8,12},{10,14},{12,8},{14,10},{16,20},{18,... | collective-permute-start | bytes 98312 | tf_op jit(solution)/shard_map/ppermute | solution.py:258
  33.6 1.5 %collective-permute-start.3 = (f32[64,128]{1,0:T(8,128)S(1)}, f32[64,128]{1,0:T(8,128)S(1)}, u32[]{:S(2)}, u32[]{:S(2)}) collective-permute-start(f32[64,128]{1,0:T(8,128)S(1)} %shard_map.91.vec.previous.first), channel_id=1, source_target_pairs={{0,2},{2,0},{4,6},{6,4},{8,10},{10,8},{12,14},{14,12},{16,18},{18,... | collective-permute-start | bytes 98312 | tf_op jit(solution)/shard_map/ppermute | solution.py:258
  35.1 1.2 %copy-done.5 = bf16[1,64,64,128]{3,2,1,0:T(8,128)(2,1)S(1)} copy-done((bf16[1,64,64,128]{3,2,1,0:T(8,128)(2,1)S(1)}, bf16[1,64,64,128]{3,2,1,0:T(8,128)(2,1)}, u32[]{:S(2)}) %copy-start.5) | copy-done | bytes 1048600
  36.6 1.6 %copy-done.11 = bf16[1,2,64,64,128]{4,3,2,1,0:T(8,128)(2,1)S(1)} copy-done((bf16[1,2,64,64,128]{4,3,2,1,0:T(8,128)(2,1)S(1)}, bf16[1,2,64,64,128]{4,3,2,1,0:T(8,128)(2,1)}, u32[]{:S(2)}) %copy-start.11) | copy-done | bytes 2097176
  38.9 0.7 shard_map.93.known
  41.5 1.2 %copy-done.6 = bf16[1,64,64,128]{3,2,1,0:T(8,128)(2,1)S(1)} copy-done((bf16[1,64,64,128]{3,2,1,0:T(8,128)(2,1)S(1)}, bf16[1,64,64,128]{3,2,1,0:T(8,128)(2,1)}, u32[]{:S(2)}) %copy-start.6) | copy-done | bytes 1048600
  42.7 1.2 %copy-done.19 = bf16[1,64,64,96]{3,2,1,0:T(8,128)(2,1)S(1)} copy-done((bf16[1,64,64,96]{3,2,1,0:T(8,128)(2,1)S(1)}, bf16[1,64,64,96]{3,2,1,0:T(8,128)(2,1)}, u32[]{:S(2)}) %copy-start.19) | copy-done | bytes 786456
  43.9 0.8 copy-done.42
  44.7 0.8 copy-done.44
  45.4 0.8 copy-done.46
  46.2 1.8 %shard_map.94 = (f32[64,128]{1,0:T(8,128)S(1)}, f32[64,128]{1,0:T(8,128)S(1)}, f32[32,8,128]{2,1,0:T(8,128)}, f32[32,128]{1,0:T(8,128)}) custom-call(f32[64,128]{1,0:T(8,128)S(1)} %shard_map.93.known, f32[64,128]{1,0:T(8,128)S(1)} %copy-done.46, f32[64,128]{1,0:T(8,128)S(1)} %copy-done.44, f32[64,128]{1,0:T(8,128)S(1)} %copy-done.42, ...), custom_call_target="tpu_custom_call" | custom-call | flops 2359296 | bytes 2523136 | tf_op jit(solution)/shard_map/pallas_call | solution.py:23
  47.9 2.8 %all-to-all-start.1 = ((f32[32,8,128]{2,1,0:T(8,128)}), f32[32,8,128]{2,1,0:T(8,128)S(1)}, u32[]{:S(2)}, u32[]{:S(2)}) async-start(f32[32,8,128]{2,1,0:T(8,128)} %get-tuple-element.26), calls=%async_computation.1 | async-start | bytes 262144 | tf_op jit(solution)/shard_map/all_to_all | solution.py:244
  51.1 1.2 %copy-done.7 = bf16[1,64,64,128]{3,2,1,0:T(8,128)(2,1)S(1)} copy-done((bf16[1,64,64,128]{3,2,1,0:T(8,128)(2,1)S(1)}, bf16[1,64,64,128]{3,2,1,0:T(8,128)(2,1)}, u32[]{:S(2)}) %copy-start.7) | copy-done | bytes 1048600
  52.7 1.6 %copy-done.12 = bf16[1,2,64,64,128]{4,3,2,1,0:T(8,128)(2,1)S(1)} copy-done((bf16[1,2,64,64,128]{4,3,2,1,0:T(8,128)(2,1)S(1)}, bf16[1,2,64,64,128]{4,3,2,1,0:T(8,128)(2,1)}, u32[]{:S(2)}) %copy-start.12) | copy-done | bytes 2097176
  54.3 0.8 copy-done.28
  55.0 0.8 copy-done.32
  56.4 1.6 %shard_map.96 = (f32[64,128]{1,0:T(8,128)S(1)}, f32[64,128]{1,0:T(8,128)}) custom-call(f32[64,128]{1,0:T(8,128)S(1)} %copy-done.32, f32[1,64,128]{2,1,0:T(8,128)S(1)} %bitcast.53, f32[64,128]{1,0:T(8,128)S(1)} %shard_map.95.own, f32[64,128]{1,0:T(8,128)S(1)} %copy-done.28, bf16[64,64,128]{2,1,0:T(8,128)(2,1)S(1)} %bitcast.24, ...), custom_call_target="tpu_custom_call" | custom-call | flops 3145728 | bytes 3277824 | tf_op jit(solution)/shard_map/pallas_call | solution.py:23
  59.9 1.6 %copy-done.13 = bf16[1,2,64,64,128]{4,3,2,1,0:T(8,128)(2,1)S(1)} copy-done((bf16[1,2,64,64,128]{4,3,2,1,0:T(8,128)(2,1)S(1)}, bf16[1,2,64,64,128]{4,3,2,1,0:T(8,128)(2,1)}, u32[]{:S(2)}) %copy-start.13) | copy-done | bytes 2097176
  61.5 0.8 copy-done.36
  62.2 0.8 copy-done.48
  63.0 1.6 %shard_map.98 = (f32[64,128]{1,0:T(8,128)S(1)}, f32[64,128]{1,0:T(8,128)}) custom-call(f32[64,128]{1,0:T(8,128)S(1)} %copy-done.36, f32[1,64,128]{2,1,0:T(8,128)S(1)} %bitcast.56, f32[64,128]{1,0:T(8,128)S(1)} %shard_map.97.own, f32[64,128]{1,0:T(8,128)S(1)} %copy-done.28, bf16[64,64,128]{2,1,0:T(8,128)(2,1)S(1)} %bitcast.26, ...), custom_call_target="tpu_custom_call" | custom-call | flops 3145728 | bytes 3277824 | tf_op jit(solution)/shard_map/pallas_call | solution.py:23
  65.2 1.0 %copy-done.18 = bf16[1,32,64,128]{3,2,1,0:T(8,128)(2,1)S(1)} copy-done((bf16[1,32,64,128]{3,2,1,0:T(8,128)(2,1)S(1)}, bf16[1,32,64,128]{3,2,1,0:T(8,128)(2,1)}, u32[]{:S(2)}) %copy-start.18) | copy-done | bytes 524312
  66.3 0.8 copy-done.30
  67.1 0.8 copy-done.52
  68.4 1.8 %collective-permute-start.11 = (f32[64,128]{1,0:T(8,128)S(1)}, f32[64,128]{1,0:T(8,128)S(1)}, u32[]{:S(2)}, u32[]{:S(2)}) collective-permute-start(f32[64,128]{1,0:T(8,128)S(1)} %get-tuple-element.27.vec.second), channel_id=1, source_target_pairs={{0,8},{2,10},{4,12},{6,14},{8,0},{10,2},{12,4},{14,6},{16,24},{18,... | collective-permute-start | bytes 98312 | tf_op jit(solution)/shard_map/ppermute | solution.py:258
  70.2 1.5 %collective-permute-start.10 = (f32[64,128]{1,0:T(8,128)S(1)}, f32[64,128]{1,0:T(8,128)S(1)}, u32[]{:S(2)}, u32[]{:S(2)}) collective-permute-start(f32[64,128]{1,0:T(8,128)S(1)} %get-tuple-element.27.vec.second), channel_id=1, source_target_pairs={{0,4},{2,6},{4,0},{6,2},{8,12},{10,14},{12,8},{14,10},{16,20},{18,... | collective-permute-start | bytes 98312 | tf_op jit(solution)/shard_map/ppermute | solution.py:258
  71.6 1.5 %collective-permute-start.9 = (f32[64,128]{1,0:T(8,128)S(1)}, f32[64,128]{1,0:T(8,128)S(1)}, u32[]{:S(2)}, u32[]{:S(2)}) collective-permute-start(f32[64,128]{1,0:T(8,128)S(1)} %get-tuple-element.27.vec.second), channel_id=1, source_target_pairs={{0,2},{2,0},{4,6},{6,4},{8,10},{10,8},{12,14},{14,12},{16,18},{18,... | collective-permute-start | bytes 98312 | tf_op jit(solution)/shard_map/ppermute | solution.py:258
  73.1 1.2 %copy-done.8 = bf16[1,64,64,128]{3,2,1,0:T(8,128)(2,1)S(1)} copy-done((bf16[1,64,64,128]{3,2,1,0:T(8,128)(2,1)S(1)}, bf16[1,64,64,128]{3,2,1,0:T(8,128)(2,1)}, u32[]{:S(2)}) %copy-start.8) | copy-done | bytes 1048600
  74.7 1.6 %copy-done.14 = bf16[1,2,64,64,128]{4,3,2,1,0:T(8,128)(2,1)S(1)} copy-done((bf16[1,2,64,64,128]{4,3,2,1,0:T(8,128)(2,1)S(1)}, bf16[1,2,64,64,128]{4,3,2,1,0:T(8,128)(2,1)}, u32[]{:S(2)}) %copy-start.14) | copy-done | bytes 2097176
  77.5 10.9 %all_to_all.15.arrived = f32[32,8,128]{2,1,0:T(8,128)S(1)} all-to-all(f32[32,8,128]{2,1,0:T(8,128)S(1)} %get-tuple-element.29), channel_id=1, replica_groups=mesh['sub'=16,'coarse'=2] {'sub','coarse'}, dimensions={0} | all-to-all | bytes 262144 | tf_op jit(solution)/shard_map/all_to_all | solution.py:244
  (107 shorter events, 13.6 us)
Async XLA Ops:
  0.6 13.0 %copy-start.37 = (s32[1,2,128]{2,1,0:T(2,128)S(1)}, s32[1,2,128]{2,1,0:T(2,128)}, u32[]{:S(2)}) copy-start(s32[1,2,128]{2,1,0:T(2,128)} %param.11) | copy-start | bytes 3076
  0.6 1.2 %copy-start = (bf16[1,64,64,128]{3,2,1,0:T(8,128)(2,1)S(1)}, bf16[1,64,64,128]{3,2,1,0:T(8,128)(2,1)}, u32[]{:S(2)}) copy-start(bf16[1,64,64,128]{3,2,1,0:T(8,128)(2,1)} %param.9) | copy-start | bytes 3145732
  1.9 1.0 %copy-start.15 = (bf16[1,32,64,128]{3,2,1,0:T(8,128)(2,1)S(1)}, bf16[1,32,64,128]{3,2,1,0:T(8,128)(2,1)}, u32[]{:S(2)}) copy-start(bf16[1,32,64,128]{3,2,1,0:T(8,128)(2,1)} %param.12) | copy-start | bytes 1572868
  2.9 0.8 copy-start.21
  3.7 9.0 %copy-start.1 = (bf16[1,64,64,128]{3,2,1,0:T(8,128)(2,1)S(1)}, bf16[1,64,64,128]{3,2,1,0:T(8,128)(2,1)}, u32[]{:S(2)}) copy-start(bf16[1,64,64,128]{3,2,1,0:T(8,128)(2,1)} %param.9) | copy-start | bytes 3145732
  5.0 20.6 %all-to-all-start = ((f32[32,8,128]{2,1,0:T(8,128)}), f32[32,8,128]{2,1,0:T(8,128)S(1)}, u32[]{:S(2)}, u32[]{:S(2)}) async-start(f32[32,8,128]{2,1,0:T(8,128)} %get-tuple-element.21), calls=%async_computation | async-start | bytes 262144 | tf_op jit(solution)/shard_map/all_to_all | solution.py:244
  12.3 1.3 %collective-permute-start = (f32[64,128]{1,0:T(8,128)S(1)}, f32[64,128]{1,0:T(8,128)S(1)}, u32[]{:S(2)}, u32[]{:S(2)}) collective-permute-start(f32[64,128]{1,0:T(8,128)S(1)} %get-tuple-element.18.vec.state), channel_id=1, source_target_pairs={{0,1},{1,0},{2,3},{3,2},{4,5},{5,4},{6,7},{7,6},{8,9},{9,8},{10,11... | collective-permute-start | bytes 98312 | tf_op jit(solution)/shard_map/ppermute | solution.py:229
  13.6 1.2 %copy-start.2 = (bf16[1,64,64,128]{3,2,1,0:T(8,128)(2,1)S(1)}, bf16[1,64,64,128]{3,2,1,0:T(8,128)(2,1)}, u32[]{:S(2)}) copy-start(bf16[1,64,64,128]{3,2,1,0:T(8,128)(2,1)} %param.9) | copy-start | bytes 3145732
  14.8 1.6 %copy-start.9 = (bf16[1,2,64,64,128]{4,3,2,1,0:T(8,128)(2,1)S(1)}, bf16[1,2,64,64,128]{4,3,2,1,0:T(8,128)(2,1)}, u32[]{:S(2)}) copy-start(bf16[1,2,64,64,128]{4,3,2,1,0:T(8,128)(2,1)} %param.8) | copy-start | bytes 6291460
  16.4 3.4 %copy-start.22 = (f32[1,64,128]{2,1,0:T(8,128)S(1)}, f32[1,64,128]{2,1,0:T(8,128)}, u32[]{:S(2)}) copy-start(f32[1,64,128]{2,1,0:T(8,128)} %param.7) | copy-start | bytes 98308
  18.0 1.8 %copy-start.33 = (f32[64,128]{1,0:T(8,128)}, f32[64,128]{1,0:T(8,128)S(1)}, u32[]{:S(2)}) copy-start(f32[64,128]{1,0:T(8,128)S(1)} %get-tuple-element.19.vec.state) | copy-start | bytes 98308
  18.0 1.8 %collective-permute-start.1 = (f32[64,128]{1,0:T(8,128)S(1)}, f32[64,128]{1,0:T(8,128)S(1)}, u32[]{:S(2)}, u32[]{:S(2)}) collective-permute-start(f32[64,128]{1,0:T(8,128)S(1)} %get-tuple-element.19.vec.state), channel_id=1, source_target_pairs={{0,1},{1,0},{2,3},{3,2},{4,5},{5,4},{6,7},{7,6},{8,9},{9,8},{10,11... | collective-permute-start | bytes 98312 | tf_op jit(solution)/shard_map/ppermute | solution.py:229
  18.3 1.2 %copy-start.3 = (bf16[1,64,64,128]{3,2,1,0:T(8,128)(2,1)S(1)}, bf16[1,64,64,128]{3,2,1,0:T(8,128)(2,1)}, u32[]{:S(2)}) copy-start(bf16[1,64,64,128]{3,2,1,0:T(8,128)(2,1)} %param.9) | copy-start | bytes 3145732
  19.8 1.2 %copy-start.4 = (bf16[1,64,64,128]{3,2,1,0:T(8,128)(2,1)S(1)}, bf16[1,64,64,128]{3,2,1,0:T(8,128)(2,1)}, u32[]{:S(2)}) copy-start(bf16[1,64,64,128]{3,2,1,0:T(8,128)(2,1)} %param.9) | copy-start | bytes 3145732
  21.1 1.6 %copy-start.10 = (bf16[1,2,64,64,128]{4,3,2,1,0:T(8,128)(2,1)S(1)}, bf16[1,2,64,64,128]{4,3,2,1,0:T(8,128)(2,1)}, u32[]{:S(2)}) copy-start(bf16[1,2,64,64,128]{4,3,2,1,0:T(8,128)(2,1)} %param.8) | copy-start | bytes 6291460
  26.3 1.0 %copy-start.16 = (bf16[1,32,64,128]{3,2,1,0:T(8,128)(2,1)S(1)}, bf16[1,32,64,128]{3,2,1,0:T(8,128)(2,1)}, u32[]{:S(2)}) copy-start(bf16[1,32,64,128]{3,2,1,0:T(8,128)(2,1)} %param.12) | copy-start | bytes 1572868
  27.3 0.9 %copy-start.26 = (f32[32,8,128]{2,1,0:T(8,128)S(1)}, f32[32,8,128]{2,1,0:T(8,128)}, u32[]{:S(2)}) copy-start(f32[32,8,128]{2,1,0:T(8,128)} %copy-done.25) | copy-start | bytes 393220
  28.2 0.8 copy-start.29
  29.8 11.6 %copy-start.17 = (bf16[1,32,64,128]{3,2,1,0:T(8,128)(2,1)S(1)}, bf16[1,32,64,128]{3,2,1,0:T(8,128)(2,1)}, u32[]{:S(2)}) copy-start(bf16[1,32,64,128]{3,2,1,0:T(8,128)(2,1)} %param.12) | copy-start | bytes 1572868
  30.0 10.8 %copy-start.23 = (f32[64,128]{1,0:T(8,128)}, f32[64,128]{1,0:T(8,128)S(1)}, u32[]{:S(2)}) copy-start(f32[64,128]{1,0:T(8,128)S(1)} %shard_map.91.vec.previous.first) | copy-start | bytes 98308
  30.1 6.6 %collective-permute-start.2 = (f32[64,128]{1,0:T(8,128)S(1)}, f32[64,128]{1,0:T(8,128)S(1)}, u32[]{:S(2)}, u32[]{:S(2)}) collective-permute-start(f32[64,128]{1,0:T(8,128)S(1)} %shard_map.91.vec.previous.first), channel_id=1, source_target_pairs={{0,1},{1,0},{2,3},{3,2},{4,5},{5,4},{6,7},{7,6},{8,9},{9,8},{10,11... | collective-permute-start | bytes 98312 | tf_op jit(solution)/shard_map/ppermute | solution.py:229
  30.4 9.2 %collective-permute-start.5 = (f32[64,128]{1,0:T(8,128)S(1)}, f32[64,128]{1,0:T(8,128)S(1)}, u32[]{:S(2)}, u32[]{:S(2)}) collective-permute-start(f32[64,128]{1,0:T(8,128)S(1)} %shard_map.91.vec.previous.first), channel_id=1, source_target_pairs={{0,8},{2,10},{4,12},{6,14},{8,0},{10,2},{12,4},{14,6},{16,24},{18,... | collective-permute-start | bytes 98312 | tf_op jit(solution)/shard_map/ppermute | solution.py:258
  32.2 8.1 %collective-permute-start.4 = (f32[64,128]{1,0:T(8,128)S(1)}, f32[64,128]{1,0:T(8,128)S(1)}, u32[]{:S(2)}, u32[]{:S(2)}) collective-permute-start(f32[64,128]{1,0:T(8,128)S(1)} %shard_map.91.vec.previous.first), channel_id=1, source_target_pairs={{0,4},{2,6},{4,0},{6,2},{8,12},{10,14},{12,8},{14,10},{16,20},{18,... | collective-permute-start | bytes 98312 | tf_op jit(solution)/shard_map/ppermute | solution.py:258
  33.6 7.2 %collective-permute-start.3 = (f32[64,128]{1,0:T(8,128)S(1)}, f32[64,128]{1,0:T(8,128)S(1)}, u32[]{:S(2)}, u32[]{:S(2)}) collective-permute-start(f32[64,128]{1,0:T(8,128)S(1)} %shard_map.91.vec.previous.first), channel_id=1, source_target_pairs={{0,2},{2,0},{4,6},{6,4},{8,10},{10,8},{12,14},{14,12},{16,18},{18,... | collective-permute-start | bytes 98312 | tf_op jit(solution)/shard_map/ppermute | solution.py:258
  35.1 1.2 %copy-start.5 = (bf16[1,64,64,128]{3,2,1,0:T(8,128)(2,1)S(1)}, bf16[1,64,64,128]{3,2,1,0:T(8,128)(2,1)}, u32[]{:S(2)}) copy-start(bf16[1,64,64,128]{3,2,1,0:T(8,128)(2,1)} %param.9) | copy-start | bytes 3145732
  36.6 1.6 %copy-start.11 = (bf16[1,2,64,64,128]{4,3,2,1,0:T(8,128)(2,1)S(1)}, bf16[1,2,64,64,128]{4,3,2,1,0:T(8,128)(2,1)}, u32[]{:S(2)}) copy-start(bf16[1,2,64,64,128]{4,3,2,1,0:T(8,128)(2,1)} %param.8) | copy-start | bytes 6291460
  41.5 1.2 %copy-start.6 = (bf16[1,64,64,128]{3,2,1,0:T(8,128)(2,1)S(1)}, bf16[1,64,64,128]{3,2,1,0:T(8,128)(2,1)}, u32[]{:S(2)}) copy-start(bf16[1,64,64,128]{3,2,1,0:T(8,128)(2,1)} %param.9) | copy-start | bytes 3145732
  42.7 1.2 %copy-start.19 = (bf16[1,64,64,96]{3,2,1,0:T(8,128)(2,1)S(1)}, bf16[1,64,64,96]{3,2,1,0:T(8,128)(2,1)}, u32[]{:S(2)}) copy-start(bf16[1,64,64,96]{3,2,1,0:T(8,128)(2,1)} %param.10) | copy-start | bytes 2359300
  47.9 2.8 %copy-start.27 = (f32[64,128]{1,0:T(8,128)}, f32[64,128]{1,0:T(8,128)S(1)}, u32[]{:S(2)}) copy-start(f32[64,128]{1,0:T(8,128)S(1)} %get-tuple-element.23.resid.image) | copy-start | bytes 98308
  47.9 4.7 %copy-start.31 = (f32[64,128]{1,0:T(8,128)}, f32[64,128]{1,0:T(8,128)S(1)}, u32[]{:S(2)}) copy-start(f32[64,128]{1,0:T(8,128)S(1)} %get-tuple-element.22.vec.state) | copy-start | bytes 98308
  47.9 17.3 %all-to-all-start.1 = ((f32[32,8,128]{2,1,0:T(8,128)}), f32[32,8,128]{2,1,0:T(8,128)S(1)}, u32[]{:S(2)}, u32[]{:S(2)}) async-start(f32[32,8,128]{2,1,0:T(8,128)} %get-tuple-element.26), calls=%async_computation.1 | async-start | bytes 262144 | tf_op jit(solution)/shard_map/all_to_all | solution.py:244
  50.8 1.9 %collective-permute-start.6 = (f32[64,128]{1,0:T(8,128)S(1)}, f32[64,128]{1,0:T(8,128)S(1)}, u32[]{:S(2)}, u32[]{:S(2)}) collective-permute-start(f32[64,128]{1,0:T(8,128)S(1)} %get-tuple-element.22.vec.state), channel_id=1, source_target_pairs={{0,1},{1,0},{2,3},{3,2},{4,5},{5,4},{6,7},{7,6},{8,9},{9,8},{10,11... | collective-permute-start | bytes 98312 | tf_op jit(solution)/shard_map/ppermute | solution.py:229
  51.1 1.2 %copy-start.7 = (bf16[1,64,64,128]{3,2,1,0:T(8,128)(2,1)S(1)}, bf16[1,64,64,128]{3,2,1,0:T(8,128)(2,1)}, u32[]{:S(2)}) copy-start(bf16[1,64,64,128]{3,2,1,0:T(8,128)(2,1)} %param.9) | copy-start | bytes 3145732
  52.7 1.6 %copy-start.12 = (bf16[1,2,64,64,128]{4,3,2,1,0:T(8,128)(2,1)S(1)}, bf16[1,2,64,64,128]{4,3,2,1,0:T(8,128)(2,1)}, u32[]{:S(2)}) copy-start(bf16[1,2,64,64,128]{4,3,2,1,0:T(8,128)(2,1)} %param.8) | copy-start | bytes 6291460
  58.1 1.2 %copy-start.35 = (f32[64,128]{1,0:T(8,128)}, f32[64,128]{1,0:T(8,128)S(1)}, u32[]{:S(2)}) copy-start(f32[64,128]{1,0:T(8,128)S(1)} %get-tuple-element.24.vec.state) | copy-start | bytes 98308
  58.1 7.2 %copy-start.24 = (f32[64,128]{1,0:T(8,128)S(1)}, f32[64,128]{1,0:T(8,128)}, u32[]{:S(2)}) copy-start(f32[64,128]{1,0:T(8,128)} %copy-done.23) | copy-start | bytes 98308
  58.1 1.2 %collective-permute-start.7 = (f32[64,128]{1,0:T(8,128)S(1)}, f32[64,128]{1,0:T(8,128)S(1)}, u32[]{:S(2)}, u32[]{:S(2)}) collective-permute-start(f32[64,128]{1,0:T(8,128)S(1)} %get-tuple-element.24.vec.state), channel_id=1, source_target_pairs={{0,1},{1,0},{2,3},{3,2},{4,5},{5,4},{6,7},{7,6},{8,9},{9,8},{10,11... | collective-permute-start | bytes 98312 | tf_op jit(solution)/shard_map/ppermute | solution.py:229
  59.9 1.6 %copy-start.13 = (bf16[1,2,64,64,128]{4,3,2,1,0:T(8,128)(2,1)S(1)}, bf16[1,2,64,64,128]{4,3,2,1,0:T(8,128)(2,1)}, u32[]{:S(2)}) copy-start(bf16[1,2,64,64,128]{4,3,2,1,0:T(8,128)(2,1)} %param.8) | copy-start | bytes 6291460
  63.0 11.7 %copy-start.40 = (s32[1,2,128]{2,1,0:T(2,128)S(1)}, s32[1,2,128]{2,1,0:T(2,128)}, u32[]{:S(2)}) copy-start(s32[1,2,128]{2,1,0:T(2,128)} %param.11) | copy-start | bytes 3076
  65.2 1.0 %copy-start.18 = (bf16[1,32,64,128]{3,2,1,0:T(8,128)(2,1)S(1)}, bf16[1,32,64,128]{3,2,1,0:T(8,128)(2,1)}, u32[]{:S(2)}) copy-start(bf16[1,32,64,128]{3,2,1,0:T(8,128)(2,1)} %param.12) | copy-start | bytes 1572868
  66.3 0.8 copy-start.30
  68.1 6.6 %collective-permute-start.8 = (f32[64,128]{1,0:T(8,128)S(1)}, f32[64,128]{1,0:T(8,128)S(1)}, u32[]{:S(2)}, u32[]{:S(2)}) collective-permute-start(f32[64,128]{1,0:T(8,128)S(1)} %get-tuple-element.27.vec.second), channel_id=1, source_target_pairs={{0,1},{1,0},{2,3},{3,2},{4,5},{5,4},{6,7},{7,6},{8,9},{9,8},{10,11... | collective-permute-start | bytes 98312 | tf_op jit(solution)/shard_map/ppermute | solution.py:229
  68.4 8.5 %collective-permute-start.11 = (f32[64,128]{1,0:T(8,128)S(1)}, f32[64,128]{1,0:T(8,128)S(1)}, u32[]{:S(2)}, u32[]{:S(2)}) collective-permute-start(f32[64,128]{1,0:T(8,128)S(1)} %get-tuple-element.27.vec.second), channel_id=1, source_target_pairs={{0,8},{2,10},{4,12},{6,14},{8,0},{10,2},{12,4},{14,6},{16,24},{18,... | collective-permute-start | bytes 98312 | tf_op jit(solution)/shard_map/ppermute | solution.py:258
  70.2 6.8 %collective-permute-start.10 = (f32[64,128]{1,0:T(8,128)S(1)}, f32[64,128]{1,0:T(8,128)S(1)}, u32[]{:S(2)}, u32[]{:S(2)}) collective-permute-start(f32[64,128]{1,0:T(8,128)S(1)} %get-tuple-element.27.vec.second), channel_id=1, source_target_pairs={{0,4},{2,6},{4,0},{6,2},{8,12},{10,14},{12,8},{14,10},{16,20},{18,... | collective-permute-start | bytes 98312 | tf_op jit(solution)/shard_map/ppermute | solution.py:258
  71.6 5.3 %collective-permute-start.9 = (f32[64,128]{1,0:T(8,128)S(1)}, f32[64,128]{1,0:T(8,128)S(1)}, u32[]{:S(2)}, u32[]{:S(2)}) collective-permute-start(f32[64,128]{1,0:T(8,128)S(1)} %get-tuple-element.27.vec.second), channel_id=1, source_target_pairs={{0,2},{2,0},{4,6},{6,4},{8,10},{10,8},{12,14},{14,12},{16,18},{18,... | collective-permute-start | bytes 98312 | tf_op jit(solution)/shard_map/ppermute | solution.py:258
  73.1 1.2 %copy-start.8 = (bf16[1,64,64,128]{3,2,1,0:T(8,128)(2,1)S(1)}, bf16[1,64,64,128]{3,2,1,0:T(8,128)(2,1)}, u32[]{:S(2)}) copy-start(bf16[1,64,64,128]{3,2,1,0:T(8,128)(2,1)} %param.9) | copy-start | bytes 3145732
  74.3 2.6 %copy-start.20 = (bf16[1,64,64,96]{3,2,1,0:T(8,128)(2,1)S(1)}, bf16[1,64,64,96]{3,2,1,0:T(8,128)(2,1)}, u32[]{:S(2)}) copy-start(bf16[1,64,64,96]{3,2,1,0:T(8,128)(2,1)} %param.10) | copy-start | bytes 2359300
  74.7 1.6 %copy-start.14 = (bf16[1,2,64,64,128]{4,3,2,1,0:T(8,128)(2,1)S(1)}, bf16[1,2,64,64,128]{4,3,2,1,0:T(8,128)(2,1)}, u32[]{:S(2)}) copy-start(bf16[1,2,64,64,128]{4,3,2,1,0:T(8,128)(2,1)} %param.8) | copy-start | bytes 6291460
  (19 other events, 13.3 us)
where the time goes:
time: 91.4 us; the launch traced here: 89.7 us
  local copies, waits for them, and re-layouts  41.5 us (45%)
  starting transfers between devices  21.3 us (23%)
  Pallas kernels  13.7 us (15%)
  blocking collectives  10.9 us (12%)
  waiting for transfers between devices  1.32 us (1%)
  between operations  0.96 us (1%)
    unnamed x108, local copies, waits for them, and re-layouts  41.5 us
    pallas_call x18, Pallas kernels, call(): pl.pallas_call(body, out_shape=[pltpu.VMEM(shape, jnp.float32) for shape...  13.7 us
    all_to_all x1, blocking collectives, everywhere(): return lax.all_to_all(message, ('sub', 'coarse'), 0, 0)  10.9 us
    all_to_all x2, starting transfers between devices, everywhere(): return lax.all_to_all(message, ('sub', 'coarse'), 0, 0)  10.1 us
    ppermute x6, starting transfers between devices, apply(): lax.ppermute(vec, 'sub', swap(subs, 1 << bit))  9.4 us
  transfers between devices with their start and end apart: 14, of which 2 were waited for; matrix products, arithmetic and copies ran while one was open for 0% of the time, Pallas kernels for 11%

commit v1 on v0

--- a/solution.py
+++ b/solution.py
@@ -10,6 +10,7 @@
 SWEEPS = 3
 ITERS = 2
 ROWS = 8
+SCOPED = 2 << 20
 HIGH = lax.Precision.HIGHEST
 
 
@@ -26,6 +27,7 @@
         in_specs=[pl.BlockSpec(memory_space=pltpu.VMEM) for _ in args],
         out_specs=[pl.BlockSpec(memory_space=pltpu.VMEM) for _ in outs],
         cost_estimate=pl.CostEstimate(flops=2 * macs, bytes_accessed=size, transcendentals=0),
+        compiler_params=pltpu.CompilerParams(vmem_limit_bytes=SCOPED),
     )(*args)
 
 

time: 91.4 us -> 62.6 us (0.68); the launches traced: 89.7 us -> 62.1 us
  local copies, waits for them, and re-layouts: 41.5 us -> 8.6 us
  waiting for transfers between devices: 1.32 us -> 9.47 us
  starting transfers between devices: 21.3 us -> 18.5 us
    unnamed x108 -> x32, local copies, waits for them, and re-layouts: 41.5 us -> 8.6 us
    ppermute x6, starting transfers between devices: 9.4 us -> 5.82 us  [apply(): lax.ppermute(vec, 'sub', swap(subs, 1 << bit))]
    all_to_all x2, waiting for transfers between devices: 0.01 us -> 3.47 us  [everywhere(): return lax.all_to_all(message, ('sub', 'coarse'), 0, 0)]
    ppermute x6, waiting for transfers between devices: 0.02 us -> 3.4 us  [apply(): lax.ppermute(vec, 'sub', swap(subs, 1 << bit))]
    ppermute x6, waiting for transfers between devices: 1.3 us -> 2.6 us  [gathered(): return lax.ppermute(vec, 'coarse', swap(2, 1))[None]]
  transfers between devices with their start and end apart: 14 -> 14, of which waited for: 2 -> 10; matrix products, arithmetic and copies ran while one was open for 0% -> 0% of each run, Pallas kernels for 11% -> 15%
where the time goes in v1:
time: 62.6 us; the launch traced here: 62.1 us
  starting transfers between devices  18.5 us (30%)
  Pallas kernels  13.4 us (21%)
  blocking collectives  11.2 us (18%)
  waiting for transfers between devices  9.47 us (15%)
  local copies, waits for them, and re-layouts  8.6 us (14%)
  between operations  0.8 us (1%)
    pallas_call x18, Pallas kernels, call(): pl.pallas_call(body, out_shape=[pltpu.VMEM(shape, jnp.float32) for shape...  13.4 us
    all_to_all x1, blocking collectives, everywhere(): return lax.all_to_all(message, ('sub', 'coarse'), 0, 0)  11.2 us
    all_to_all x2, starting transfers between devices, everywhere(): return lax.all_to_all(message, ('sub', 'coarse'), 0, 0)  11 us
    unnamed x32, local copies, waits for them, and re-layouts  8.6 us
    ppermute x6, starting transfers between devices, apply(): lax.ppermute(vec, 'sub', swap(subs, 1 << bit))  5.82 us
    all_to_all x2, waiting for transfers between devices, everywhere(): return lax.all_to_all(message, ('sub', 'coarse'), 0, 0)  3.47 us
    ppermute x6, waiting for transfers between devices, apply(): lax.ppermute(vec, 'sub', swap(subs, 1 << bit))  3.4 us
    ppermute x6, waiting for transfers between devices, gathered(): return lax.ppermute(vec, 'coarse', swap(2, 1))[None]  2.6 us
  transfers between devices with their start and end apart: 14, of which 10 were waited for; matrix products, arithmetic and copies ran while one was open for 0% of the time, Pallas kernels for 15%

profile of v1, /device:TPU:0, one launch (start us, length us, event | category | flops | bytes accessed | tf_op | source)
XLA Modules:
  0.0 62.1 jit_solution(15077063168374547722)
XLA Ops:
  0.6 1.2 %copy-done = bf16[1,64,64,128]{3,2,1,0:T(8,128)(2,1)S(1)} copy-done((bf16[1,64,64,128]{3,2,1,0:T(8,128)(2,1)S(1)}, bf16[1,64,64,128]{3,2,1,0:T(8,128)(2,1)}, u32[]{:S(2)}) %copy-start) | copy-done | bytes 1048600
  1.9 1.0 %copy-done.4 = bf16[1,32,64,128]{3,2,1,0:T(8,128)(2,1)S(1)} copy-done((bf16[1,32,64,128]{3,2,1,0:T(8,128)(2,1)S(1)}, bf16[1,32,64,128]{3,2,1,0:T(8,128)(2,1)}, u32[]{:S(2)}) %copy-start.4) | copy-done | bytes 524312
  2.9 0.8 %copy-done.10 = f32[1,64,128]{2,1,0:T(8,128)S(1)} copy-done((f32[1,64,128]{2,1,0:T(8,128)S(1)}, f32[1,64,128]{2,1,0:T(8,128)}, u32[]{:S(2)}) %copy-start.10) | copy-done | bytes 32792
  3.7 1.3 %shard_map.86 = (f32[64,128]{1,0:T(8,128)S(1)}, f32[32,8,128]{2,1,0:T(8,128)}, f32[32,128]{1,0:T(8,128)}) custom-call(f32[64,128]{1,0:T(8,128)S(1)} %bitcast.40, bf16[64,64,128]{2,1,0:T(8,128)(2,1)S(1)} %bitcast.16, bf16[32,64,128]{2,1,0:T(8,128)(2,1)S(1)} %bitcast.34), custom_call_target="tpu_custom_call" | custom-call | flops 1572864 | bytes 1605632 | tf_op jit(solution)/shard_map/pallas_call | solution.py:24
  5.0 7.3 %all-to-all-start = ((f32[32,8,128]{2,1,0:T(8,128)}), f32[32,8,128]{2,1,0:T(8,128)S(1)}, u32[]{:S(2)}, u32[]{:S(2)}) async-start(f32[32,8,128]{2,1,0:T(8,128)} %get-tuple-element.21), calls=%async_computation | async-start | bytes 262144 | tf_op jit(solution)/shard_map/all_to_all | solution.py:246
  12.3 0.3 collective-permute-start
  12.6 0.3 shard_map.87.own
  13.0 0.6 %collective-permute-done = f32[64,128]{1,0:T(8,128)S(1)} collective-permute-done((f32[64,128]{1,0:T(8,128)S(1)}, f32[64,128]{1,0:T(8,128)S(1)}, u32[]{:S(2)}, u32[]{:S(2)}) %collective-permute-start) | collective-permute-done | bytes 32800 | tf_op jit(solution)/shard_map/ppermute | solution.py:231
  13.6 1.6 %copy-done.2 = bf16[1,2,64,64,128]{4,3,2,1,0:T(8,128)(2,1)S(1)} copy-done((bf16[1,2,64,64,128]{4,3,2,1,0:T(8,128)(2,1)S(1)}, bf16[1,2,64,64,128]{4,3,2,1,0:T(8,128)(2,1)}, u32[]{:S(2)}) %copy-start.2) | copy-done | bytes 2097176
  15.2 1.6 %shard_map.88 = (f32[64,128]{1,0:T(8,128)S(1)}, f32[64,128]{1,0:T(8,128)}) custom-call(f32[64,128]{1,0:T(8,128)S(1)} %get-tuple-element.18.vec.state, f32[1,64,128]{2,1,0:T(8,128)S(1)} %bitcast.54, f32[64,128]{1,0:T(8,128)S(1)} %shard_map.87.own, f32[64,128]{1,0:T(8,128)S(1)} %bitcast.41, bf16[64,64,128]{2,1,0:T(8,128)(2,1)S(1)} %bitcast.18, ...), custom_call_target="tpu_custom_call" | custom-call | flops 3145728 | bytes 3277824 | tf_op jit(solution)/shard_map/pallas_call | solution.py:24
  16.8 0.3 collective-permute-start.1
  17.1 0.3 shard_map.89.own
  17.4 0.6 %collective-permute-done.1 = f32[64,128]{1,0:T(8,128)S(1)} collective-permute-done((f32[64,128]{1,0:T(8,128)S(1)}, f32[64,128]{1,0:T(8,128)S(1)}, u32[]{:S(2)}, u32[]{:S(2)}) %collective-permute-start.1) | collective-permute-done | bytes 32800 | tf_op jit(solution)/shard_map/ppermute | solution.py:231
  18.0 1.6 %shard_map.90 = (f32[64,128]{1,0:T(8,128)S(1)}, f32[64,128]{1,0:T(8,128)}) custom-call(f32[64,128]{1,0:T(8,128)S(1)} %get-tuple-element.19.vec.state, f32[1,64,128]{2,1,0:T(8,128)S(1)} %bitcast.55, f32[64,128]{1,0:T(8,128)S(1)} %shard_map.89.own, f32[64,128]{1,0:T(8,128)S(1)} %bitcast.42, bf16[64,64,128]{2,1,0:T(8,128)(2,1)S(1)} %bitcast.20, ...), custom_call_target="tpu_custom_call" | custom-call | flops 3145728 | bytes 3277824 | tf_op jit(solution)/shard_map/pallas_call | solution.py:24
  19.6 0.9 %all-to-all-done.arrived = f32[32,8,128]{2,1,0:T(8,128)S(1)} async-done(((f32[32,8,128]{2,1,0:T(8,128)}), f32[32,8,128]{2,1,0:T(8,128)S(1)}, u32[]{:S(2)}, u32[]{:S(2)}) %all-to-all-start) | async-done | bytes 131104 | tf_op jit(solution)/shard_map/all_to_all | solution.py:246
  20.6 1.0 %copy-done.5 = bf16[1,32,64,128]{3,2,1,0:T(8,128)(2,1)S(1)} copy-done((bf16[1,32,64,128]{3,2,1,0:T(8,128)(2,1)S(1)}, bf16[1,32,64,128]{3,2,1,0:T(8,128)(2,1)}, u32[]{:S(2)}) %copy-start.5) | copy-done | bytes 524312
  21.8 0.3 collective-permute-start.2
  22.1 0.8 %collective-permute-start.5 = (f32[64,128]{1,0:T(8,128)S(1)}, f32[64,128]{1,0:T(8,128)S(1)}, u32[]{:S(2)}, u32[]{:S(2)}) collective-permute-start(f32[64,128]{1,0:T(8,128)S(1)} %shard_map.91.vec.previous.first), channel_id=1, source_target_pairs={{0,8},{2,10},{4,12},{6,14},{8,0},{10,2},{12,4},{14,6},{16,24},{18,... | collective-permute-start | bytes 98312 | tf_op jit(solution)/shard_map/ppermute | solution.py:260
  22.9 1.5 %collective-permute-start.4 = (f32[64,128]{1,0:T(8,128)S(1)}, f32[64,128]{1,0:T(8,128)S(1)}, u32[]{:S(2)}, u32[]{:S(2)}) collective-permute-start(f32[64,128]{1,0:T(8,128)S(1)} %shard_map.91.vec.previous.first), channel_id=1, source_target_pairs={{0,4},{2,6},{4,0},{6,2},{8,12},{10,14},{12,8},{14,10},{16,20},{18,... | collective-permute-start | bytes 98312 | tf_op jit(solution)/shard_map/ppermute | solution.py:260
  24.3 1.5 %collective-permute-start.3 = (f32[64,128]{1,0:T(8,128)S(1)}, f32[64,128]{1,0:T(8,128)S(1)}, u32[]{:S(2)}, u32[]{:S(2)}) collective-permute-start(f32[64,128]{1,0:T(8,128)S(1)} %shard_map.91.vec.previous.first), channel_id=1, source_target_pairs={{0,2},{2,0},{4,6},{6,4},{8,10},{10,8},{12,14},{14,12},{16,18},{18,... | collective-permute-start | bytes 98312 | tf_op jit(solution)/shard_map/ppermute | solution.py:260
  25.8 0.3 shard_map.92.own
  26.1 0.7 %shard_map.93.known = f32[64,128]{1,0:T(8,128)S(1)} custom-call(f32[64,128]{1,0:T(8,128)S(1)} %shard_map.91.vec.previous.first, f32[1,64,128]{2,1,0:T(8,128)S(1)} %bitcast.51, f32[64,128]{1,0:T(8,128)S(1)} %shard_map.92.own, bf16[2,64,64,128]{3,2,1,0:T(8,128)(2,1)S(1)} %bitcast.30, s32[2,128]{1,0:T(2,128)S(1)} %bitcast.47), custom_call_target="tpu_custom_call" | custom-call | flops 2097152 | bytes 2196480 | tf_op jit(solution)/shard_map/pallas_call | solution.py:24
  26.8 1.4 %collective-permute-done.3.near0 = f32[64,128]{1,0:T(8,128)S(1)} collective-permute-done((f32[64,128]{1,0:T(8,128)S(1)}, f32[64,128]{1,0:T(8,128)S(1)}, u32[]{:S(2)}, u32[]{:S(2)}) %collective-permute-start.3) | collective-permute-done | bytes 32800 | tf_op jit(solution)/shard_map/ppermute | solution.py:260
  28.3 1.5 %shard_map.94 = (f32[64,128]{1,0:T(8,128)S(1)}, f32[64,128]{1,0:T(8,128)S(1)}, f32[32,8,128]{2,1,0:T(8,128)S(1)}, f32[32,128]{1,0:T(8,128)}) custom-call(f32[64,128]{1,0:T(8,128)S(1)} %shard_map.93.known, f32[64,128]{1,0:T(8,128)S(1)} %collective-permute-done.3.near0, f32[64,128]{1,0:T(8,128)S(1)} %collective-permute-done.4.near1, ...), custom_call_target="tpu_custom_call" | custom-call | flops 2359296 | bytes 2523136 | tf_op jit(solution)/shard_map/pallas_call | solution.py:24
  29.8 0.6 %copy-done.13 = f32[32,8,128]{2,1,0:T(8,128)} copy-done((f32[32,8,128]{2,1,0:T(8,128)}, f32[32,8,128]{2,1,0:T(8,128)S(1)}, u32[]{:S(2)}) %copy-start.13) | copy-done | bytes 131096
  30.4 3.7 %all-to-all-start.1 = ((f32[32,8,128]{2,1,0:T(8,128)}), f32[32,8,128]{2,1,0:T(8,128)S(1)}, u32[]{:S(2)}, u32[]{:S(2)}) async-start(f32[32,8,128]{2,1,0:T(8,128)} %copy-done.13), calls=%async_computation.1 | async-start | bytes 262144 | tf_op jit(solution)/shard_map/all_to_all | solution.py:246
  34.1 0.3 collective-permute-start.6
  34.4 0.3 shard_map.95.own
  34.8 0.6 %collective-permute-done.6 = f32[64,128]{1,0:T(8,128)S(1)} collective-permute-done((f32[64,128]{1,0:T(8,128)S(1)}, f32[64,128]{1,0:T(8,128)S(1)}, u32[]{:S(2)}, u32[]{:S(2)}) %collective-permute-start.6) | collective-permute-done | bytes 32800 | tf_op jit(solution)/shard_map/ppermute | solution.py:231
  35.4 1.6 %shard_map.96 = (f32[64,128]{1,0:T(8,128)S(1)}, f32[64,128]{1,0:T(8,128)}) custom-call(f32[64,128]{1,0:T(8,128)S(1)} %get-tuple-element.22.vec.state, f32[1,64,128]{2,1,0:T(8,128)S(1)} %bitcast.53, f32[64,128]{1,0:T(8,128)S(1)} %shard_map.95.own, f32[64,128]{1,0:T(8,128)S(1)} %get-tuple-element.23.resid.image, bf16[64,64,128]{2,1,0:T(8,128)(2,1)S(1)} %bitcast.24, ...), custom_call_target="tpu_custom_call" | custom-call | flops 3145728 | bytes 3277824 | tf_op jit(solution)/shard_map/pallas_call | solution.py:24
  37.3 0.3 shard_map.97.own
  37.6 0.6 %collective-permute-done.7 = f32[64,128]{1,0:T(8,128)S(1)} collective-permute-done((f32[64,128]{1,0:T(8,128)S(1)}, f32[64,128]{1,0:T(8,128)S(1)}, u32[]{:S(2)}, u32[]{:S(2)}) %collective-permute-start.7) | collective-permute-done | bytes 32800 | tf_op jit(solution)/shard_map/ppermute | solution.py:231
  38.2 1.6 %shard_map.98 = (f32[64,128]{1,0:T(8,128)S(1)}, f32[64,128]{1,0:T(8,128)}) custom-call(f32[64,128]{1,0:T(8,128)S(1)} %get-tuple-element.24.vec.state, f32[1,64,128]{2,1,0:T(8,128)S(1)} %bitcast.56, f32[64,128]{1,0:T(8,128)S(1)} %shard_map.97.own, f32[64,128]{1,0:T(8,128)S(1)} %get-tuple-element.23.resid.image, bf16[64,64,128]{2,1,0:T(8,128)(2,1)S(1)} %bitcast.26, ...), custom_call_target="tpu_custom_call" | custom-call | flops 3145728 | bytes 3277824 | tf_op jit(solution)/shard_map/pallas_call | solution.py:24
  39.8 2.5 %all-to-all-done.1.arrived = f32[32,8,128]{2,1,0:T(8,128)S(1)} async-done(((f32[32,8,128]{2,1,0:T(8,128)}), f32[32,8,128]{2,1,0:T(8,128)S(1)}, u32[]{:S(2)}, u32[]{:S(2)}) %all-to-all-start.1) | async-done | bytes 131104 | tf_op jit(solution)/shard_map/all_to_all | solution.py:246
  42.4 1.0 %copy-done.7 = bf16[1,32,64,128]{3,2,1,0:T(8,128)(2,1)S(1)} copy-done((bf16[1,32,64,128]{3,2,1,0:T(8,128)(2,1)S(1)}, bf16[1,32,64,128]{3,2,1,0:T(8,128)(2,1)}, u32[]{:S(2)}) %copy-start.7) | copy-done | bytes 524312
  43.6 0.3 collective-permute-start.8
  43.9 0.5 collective-permute-start.11
  44.4 0.7 %collective-permute-start.10 = (f32[64,128]{1,0:T(8,128)S(1)}, f32[64,128]{1,0:T(8,128)S(1)}, u32[]{:S(2)}, u32[]{:S(2)}) collective-permute-start(f32[64,128]{1,0:T(8,128)S(1)} %get-tuple-element.27.vec.second), channel_id=1, source_target_pairs={{0,4},{2,6},{4,0},{6,2},{8,12},{10,14},{12,8},{14,10},{16,20},{18,... | collective-permute-start | bytes 98312 | tf_op jit(solution)/shard_map/ppermute | solution.py:260
  45.1 0.9 %collective-permute-start.9 = (f32[64,128]{1,0:T(8,128)S(1)}, f32[64,128]{1,0:T(8,128)S(1)}, u32[]{:S(2)}, u32[]{:S(2)}) collective-permute-start(f32[64,128]{1,0:T(8,128)S(1)} %get-tuple-element.27.vec.second), channel_id=1, source_target_pairs={{0,2},{2,0},{4,6},{6,4},{8,10},{10,8},{12,14},{14,12},{16,18},{18,... | collective-permute-start | bytes 98312 | tf_op jit(solution)/shard_map/ppermute | solution.py:260
  46.0 0.3 shard_map.100.own
  46.3 0.7 %shard_map.101.known = f32[64,128]{1,0:T(8,128)S(1)} custom-call(f32[64,128]{1,0:T(8,128)S(1)} %get-tuple-element.27.vec.second, f32[1,64,128]{2,1,0:T(8,128)S(1)} %bitcast.52, f32[64,128]{1,0:T(8,128)S(1)} %shard_map.100.own, bf16[2,64,64,128]{3,2,1,0:T(8,128)(2,1)S(1)} %bitcast.33, s32[2,128]{1,0:T(2,128)S(1)} %bitcast.50), custom_call_target="tpu_custom_call" | custom-call | flops 2097152 | bytes 2196480 | tf_op jit(solution)/shard_map/pallas_call | solution.py:24
  47.0 0.8 %collective-permute-done.11.near2 = f32[64,128]{1,0:T(8,128)S(1)} collective-permute-done((f32[64,128]{1,0:T(8,128)S(1)}, f32[64,128]{1,0:T(8,128)S(1)}, u32[]{:S(2)}, u32[]{:S(2)}) %collective-permute-start.11) | collective-permute-done | bytes 32800 | tf_op jit(solution)/shard_map/ppermute | solution.py:260
  47.8 0.5 collective-permute-done.10.near1
  48.3 0.7 %collective-permute-done.9.near0 = f32[64,128]{1,0:T(8,128)S(1)} collective-permute-done((f32[64,128]{1,0:T(8,128)S(1)}, f32[64,128]{1,0:T(8,128)S(1)}, u32[]{:S(2)}, u32[]{:S(2)}) %collective-permute-start.9) | collective-permute-done | bytes 32800 | tf_op jit(solution)/shard_map/ppermute | solution.py:260
  49.0 0.6 shard_map.102
  49.5 11.2 %all_to_all.15.arrived = f32[32,8,128]{2,1,0:T(8,128)S(1)} all-to-all(f32[32,8,128]{2,1,0:T(8,128)S(1)} %get-tuple-element.29), channel_id=1, replica_groups=mesh['sub'=16,'coarse'=2] {'sub','coarse'}, dimensions={0} | all-to-all | bytes 262144 | tf_op jit(solution)/shard_map/all_to_all | solution.py:246
  60.8 0.6 copy.9
  61.4 0.6 copy.10
  (31 shorter events, 0.8 us)
Async XLA Ops:
  0.6 13.0 %copy-start.14 = (s32[1,2,128]{2,1,0:T(2,128)S(1)}, s32[1,2,128]{2,1,0:T(2,128)}, u32[]{:S(2)}) copy-start(s32[1,2,128]{2,1,0:T(2,128)} %param.11) | copy-start | bytes 3076
  0.6 1.2 %copy-start = (bf16[1,64,64,128]{3,2,1,0:T(8,128)(2,1)S(1)}, bf16[1,64,64,128]{3,2,1,0:T(8,128)(2,1)}, u32[]{:S(2)}) copy-start(bf16[1,64,64,128]{3,2,1,0:T(8,128)(2,1)} %param.9) | copy-start | bytes 3145732
  1.9 1.0 %copy-start.4 = (bf16[1,32,64,128]{3,2,1,0:T(8,128)(2,1)S(1)}, bf16[1,32,64,128]{3,2,1,0:T(8,128)(2,1)}, u32[]{:S(2)}) copy-start(bf16[1,32,64,128]{3,2,1,0:T(8,128)(2,1)} %param.12) | copy-start | bytes 1572868
  2.9 0.8 %copy-start.10 = (f32[1,64,128]{2,1,0:T(8,128)S(1)}, f32[1,64,128]{2,1,0:T(8,128)}, u32[]{:S(2)}) copy-start(f32[1,64,128]{2,1,0:T(8,128)} %param.7) | copy-start | bytes 98308
  3.7 9.0 %copy-start.1 = (bf16[1,64,64,128]{3,2,1,0:T(8,128)(2,1)S(1)}, bf16[1,64,64,128]{3,2,1,0:T(8,128)(2,1)}, u32[]{:S(2)}) copy-start(bf16[1,64,64,128]{3,2,1,0:T(8,128)(2,1)} %param.9) | copy-start | bytes 3145732
  3.7 9.9 %copy-start.11 = (f32[1,64,128]{2,1,0:T(8,128)S(1)}, f32[1,64,128]{2,1,0:T(8,128)}, u32[]{:S(2)}) copy-start(f32[1,64,128]{2,1,0:T(8,128)} %param.7) | copy-start | bytes 98308
  5.0 15.5 %all-to-all-start = ((f32[32,8,128]{2,1,0:T(8,128)}), f32[32,8,128]{2,1,0:T(8,128)S(1)}, u32[]{:S(2)}, u32[]{:S(2)}) async-start(f32[32,8,128]{2,1,0:T(8,128)} %get-tuple-element.21), calls=%async_computation | async-start | bytes 262144 | tf_op jit(solution)/shard_map/all_to_all | solution.py:246
  12.3 1.3 %collective-permute-start = (f32[64,128]{1,0:T(8,128)S(1)}, f32[64,128]{1,0:T(8,128)S(1)}, u32[]{:S(2)}, u32[]{:S(2)}) collective-permute-start(f32[64,128]{1,0:T(8,128)S(1)} %get-tuple-element.18.vec.state), channel_id=1, source_target_pairs={{0,1},{1,0},{2,3},{3,2},{4,5},{5,4},{6,7},{7,6},{8,9},{9,8},{10,11... | collective-permute-start | bytes 98312 | tf_op jit(solution)/shard_map/ppermute | solution.py:231
  13.6 1.6 %copy-start.2 = (bf16[1,2,64,64,128]{4,3,2,1,0:T(8,128)(2,1)S(1)}, bf16[1,2,64,64,128]{4,3,2,1,0:T(8,128)(2,1)}, u32[]{:S(2)}) copy-start(bf16[1,2,64,64,128]{4,3,2,1,0:T(8,128)(2,1)} %param.8) | copy-start | bytes 6291460
  15.2 2.8 %copy-start.3 = (bf16[1,2,64,64,128]{4,3,2,1,0:T(8,128)(2,1)S(1)}, bf16[1,2,64,64,128]{4,3,2,1,0:T(8,128)(2,1)}, u32[]{:S(2)}) copy-start(bf16[1,2,64,64,128]{4,3,2,1,0:T(8,128)(2,1)} %param.8) | copy-start | bytes 6291460
  16.8 3.8 %copy-start.12 = (f32[32,512]{1,0:T(8,128)S(1)}, f32[32,512]{1,0:T(8,128)}, u32[]{:S(2)}) copy-start(f32[32,512]{1,0:T(8,128)} %inverse.3) | copy-start | bytes 196612
  16.8 1.2 %collective-permute-start.1 = (f32[64,128]{1,0:T(8,128)S(1)}, f32[64,128]{1,0:T(8,128)S(1)}, u32[]{:S(2)}, u32[]{:S(2)}) collective-permute-start(f32[64,128]{1,0:T(8,128)S(1)} %get-tuple-element.19.vec.state), channel_id=1, source_target_pairs={{0,1},{1,0},{2,3},{3,2},{4,5},{5,4},{6,7},{7,6},{8,9},{9,8},{10,11... | collective-permute-start | bytes 98312 | tf_op jit(solution)/shard_map/ppermute | solution.py:231
  20.6 1.0 %copy-start.5 = (bf16[1,32,64,128]{3,2,1,0:T(8,128)(2,1)S(1)}, bf16[1,32,64,128]{3,2,1,0:T(8,128)(2,1)}, u32[]{:S(2)}) copy-start(bf16[1,32,64,128]{3,2,1,0:T(8,128)(2,1)} %param.12) | copy-start | bytes 1572868
  21.6 6.7 %copy-start.6 = (bf16[1,32,64,128]{3,2,1,0:T(8,128)(2,1)S(1)}, bf16[1,32,64,128]{3,2,1,0:T(8,128)(2,1)}, u32[]{:S(2)}) copy-start(bf16[1,32,64,128]{3,2,1,0:T(8,128)(2,1)} %param.12) | copy-start | bytes 1572868
  21.6 6.7 %copy-start.8 = (bf16[1,64,64,96]{3,2,1,0:T(8,128)(2,1)S(1)}, bf16[1,64,64,96]{3,2,1,0:T(8,128)(2,1)}, u32[]{:S(2)}) copy-start(bf16[1,64,64,96]{3,2,1,0:T(8,128)(2,1)} %param.10) | copy-start | bytes 2359300
  21.8 4.3 %collective-permute-start.2 = (f32[64,128]{1,0:T(8,128)S(1)}, f32[64,128]{1,0:T(8,128)S(1)}, u32[]{:S(2)}, u32[]{:S(2)}) collective-permute-start(f32[64,128]{1,0:T(8,128)S(1)} %shard_map.91.vec.previous.first), channel_id=1, source_target_pairs={{0,1},{1,0},{2,3},{3,2},{4,5},{5,4},{6,7},{7,6},{8,9},{9,8},{10,11... | collective-permute-start | bytes 98312 | tf_op jit(solution)/shard_map/ppermute | solution.py:231
  22.1 4.7 %collective-permute-start.5 = (f32[64,128]{1,0:T(8,128)S(1)}, f32[64,128]{1,0:T(8,128)S(1)}, u32[]{:S(2)}, u32[]{:S(2)}) collective-permute-start(f32[64,128]{1,0:T(8,128)S(1)} %shard_map.91.vec.previous.first), channel_id=1, source_target_pairs={{0,8},{2,10},{4,12},{6,14},{8,0},{10,2},{12,4},{14,6},{16,24},{18,... | collective-permute-start | bytes 98312 | tf_op jit(solution)/shard_map/ppermute | solution.py:260
  22.9 3.9 %collective-permute-start.4 = (f32[64,128]{1,0:T(8,128)S(1)}, f32[64,128]{1,0:T(8,128)S(1)}, u32[]{:S(2)}, u32[]{:S(2)}) collective-permute-start(f32[64,128]{1,0:T(8,128)S(1)} %shard_map.91.vec.previous.first), channel_id=1, source_target_pairs={{0,4},{2,6},{4,0},{6,2},{8,12},{10,14},{12,8},{14,10},{16,20},{18,... | collective-permute-start | bytes 98312 | tf_op jit(solution)/shard_map/ppermute | solution.py:260
  24.3 3.9 %collective-permute-start.3 = (f32[64,128]{1,0:T(8,128)S(1)}, f32[64,128]{1,0:T(8,128)S(1)}, u32[]{:S(2)}, u32[]{:S(2)}) collective-permute-start(f32[64,128]{1,0:T(8,128)S(1)} %shard_map.91.vec.previous.first), channel_id=1, source_target_pairs={{0,2},{2,0},{4,6},{6,4},{8,10},{10,8},{12,14},{14,12},{16,18},{18,... | collective-permute-start | bytes 98312 | tf_op jit(solution)/shard_map/ppermute | solution.py:260
  29.8 0.6 %copy-start.13 = (f32[32,8,128]{2,1,0:T(8,128)}, f32[32,8,128]{2,1,0:T(8,128)S(1)}, u32[]{:S(2)}) copy-start(f32[32,8,128]{2,1,0:T(8,128)S(1)} %get-tuple-element.26) | copy-start | bytes 393220
  30.4 12.0 %all-to-all-start.1 = ((f32[32,8,128]{2,1,0:T(8,128)}), f32[32,8,128]{2,1,0:T(8,128)S(1)}, u32[]{:S(2)}, u32[]{:S(2)}) async-start(f32[32,8,128]{2,1,0:T(8,128)} %copy-done.13), calls=%async_computation.1 | async-start | bytes 262144 | tf_op jit(solution)/shard_map/all_to_all | solution.py:246
  34.1 1.3 %collective-permute-start.6 = (f32[64,128]{1,0:T(8,128)S(1)}, f32[64,128]{1,0:T(8,128)S(1)}, u32[]{:S(2)}, u32[]{:S(2)}) collective-permute-start(f32[64,128]{1,0:T(8,128)S(1)} %get-tuple-element.22.vec.state), channel_id=1, source_target_pairs={{0,1},{1,0},{2,3},{3,2},{4,5},{5,4},{6,7},{7,6},{8,9},{9,8},{10,11... | collective-permute-start | bytes 98312 | tf_op jit(solution)/shard_map/ppermute | solution.py:231
  37.0 1.2 %collective-permute-start.7 = (f32[64,128]{1,0:T(8,128)S(1)}, f32[64,128]{1,0:T(8,128)S(1)}, u32[]{:S(2)}, u32[]{:S(2)}) collective-permute-start(f32[64,128]{1,0:T(8,128)S(1)} %get-tuple-element.24.vec.state), channel_id=1, source_target_pairs={{0,1},{1,0},{2,3},{3,2},{4,5},{5,4},{6,7},{7,6},{8,9},{9,8},{10,11... | collective-permute-start | bytes 98312 | tf_op jit(solution)/shard_map/ppermute | solution.py:231
  42.4 1.0 %copy-start.7 = (bf16[1,32,64,128]{3,2,1,0:T(8,128)(2,1)S(1)}, bf16[1,32,64,128]{3,2,1,0:T(8,128)(2,1)}, u32[]{:S(2)}) copy-start(bf16[1,32,64,128]{3,2,1,0:T(8,128)(2,1)} %param.12) | copy-start | bytes 1572868
  43.4 5.6 %copy-start.9 = (bf16[1,64,64,96]{3,2,1,0:T(8,128)(2,1)S(1)}, bf16[1,64,64,96]{3,2,1,0:T(8,128)(2,1)}, u32[]{:S(2)}) copy-start(bf16[1,64,64,96]{3,2,1,0:T(8,128)(2,1)} %param.10) | copy-start | bytes 2359300
  43.6 2.7 %collective-permute-start.8 = (f32[64,128]{1,0:T(8,128)S(1)}, f32[64,128]{1,0:T(8,128)S(1)}, u32[]{:S(2)}, u32[]{:S(2)}) collective-permute-start(f32[64,128]{1,0:T(8,128)S(1)} %get-tuple-element.27.vec.second), channel_id=1, source_target_pairs={{0,1},{1,0},{2,3},{3,2},{4,5},{5,4},{6,7},{7,6},{8,9},{9,8},{10,11... | collective-permute-start | bytes 98312 | tf_op jit(solution)/shard_map/ppermute | solution.py:231
  43.9 3.9 %collective-permute-start.11 = (f32[64,128]{1,0:T(8,128)S(1)}, f32[64,128]{1,0:T(8,128)S(1)}, u32[]{:S(2)}, u32[]{:S(2)}) collective-permute-start(f32[64,128]{1,0:T(8,128)S(1)} %get-tuple-element.27.vec.second), channel_id=1, source_target_pairs={{0,8},{2,10},{4,12},{6,14},{8,0},{10,2},{12,4},{14,6},{16,24},{18,... | collective-permute-start | bytes 98312 | tf_op jit(solution)/shard_map/ppermute | solution.py:260
  44.4 3.9 %collective-permute-start.10 = (f32[64,128]{1,0:T(8,128)S(1)}, f32[64,128]{1,0:T(8,128)S(1)}, u32[]{:S(2)}, u32[]{:S(2)}) collective-permute-start(f32[64,128]{1,0:T(8,128)S(1)} %get-tuple-element.27.vec.second), channel_id=1, source_target_pairs={{0,4},{2,6},{4,0},{6,2},{8,12},{10,14},{12,8},{14,10},{16,20},{18,... | collective-permute-start | bytes 98312 | tf_op jit(solution)/shard_map/ppermute | solution.py:260
  45.1 3.9 %collective-permute-start.9 = (f32[64,128]{1,0:T(8,128)S(1)}, f32[64,128]{1,0:T(8,128)S(1)}, u32[]{:S(2)}, u32[]{:S(2)}) collective-permute-start(f32[64,128]{1,0:T(8,128)S(1)} %get-tuple-element.27.vec.second), channel_id=1, source_target_pairs={{0,2},{2,0},{4,6},{6,4},{8,10},{10,8},{12,14},{14,12},{16,18},{18,... | collective-permute-start | bytes 98312 | tf_op jit(solution)/shard_map/ppermute | solution.py:260

commit v2 on v1

v2 whole, which is shorter than its diff:
```python
import functools

import jax
import jax.numpy as jnp
from jax import lax
from jax.experimental import pallas as pl
from jax.experimental.pallas import tpu as pltpu
from jax.sharding import PartitionSpec as P

SWEEPS = 3
ITERS = 2
ROWS = 8
SCOPED = 2 << 20
HIGH = lax.Precision.HIGHEST


def in_vmem(array):
    return pltpu.with_memory_space_constraint(array, pltpu.VMEM)


def kernel(body, outs, args, scratch=(), **kwargs):
    return pl.pallas_call(
        body,
        out_shape=outs,
        scratch_shapes=[pltpu.VMEM(shape, jnp.float32) if isinstance(shape, tuple) else shape for shape in scratch],
        cost_estimate=pl.CostEstimate(flops=0, bytes_accessed=0, transcendentals=0),
        compiler_params=pltpu.CompilerParams(vmem_limit_bytes=SCOPED),
        **kwargs,
    )(*args)


def call(body, outs, *args, keep=(), scratch=()):
    count = len(args)
    args = [in_vmem(a) for a in (*args, *keep)]

    def inner(*refs):
        body(*refs[:count], *refs[len(args) :])

    return kernel(
        inner,
        [pltpu.VMEM(shape, jnp.float32) for shape in outs],
        args,
        scratch,
        in_specs=[pl.BlockSpec(memory_space=pltpu.VMEM) for _ in args],
        out_specs=[pl.BlockSpec(memory_space=pltpu.VMEM) for _ in outs],
    )


def rows_times(blocks, vec, start):
    chunk = blocks[pl.ds(start, ROWS)].astype(jnp.float32)
    return jnp.sum(chunk * vec[None], axis=1)


def by_rows(count, body):
    def step(at, carry):
        body(pl.multiple_of(at * ROWS, ROWS))
        return carry

    lax.fori_loop(0, count // ROWS, step, 0)


def block_product(blocks, vec, out):
    def body(start):
        out[pl.ds(start, ROWS), :] = rows_times(blocks, vec, start)

    by_rows(blocks.shape[0], body)


def relaxed(dblock, vec, out, base=None):
    def body(start):
        part = dblock_rows(dblock, vec, start)
        value = part if base is None else base[pl.ds(start, ROWS), :] + part
        out[pl.ds(start, ROWS), :] = value

    whole = vec[...]

    def dblock_rows(blocks, ref, start):
        return 0.25 * (2.0 * ref[pl.ds(start, ROWS), :] - 0.25 * rows_times(blocks, whole, start))

    by_rows(dblock.shape[0], body)


def restricted(zvec, vec, scratch):
    block_product(zvec, vec, scratch)
    nvec, lanes = scratch.shape
    stacked = jnp.concatenate([scratch[...]] * (lanes // nvec), axis=0)
    ones = jnp.ones((ROWS, lanes), jnp.float32)
    return lax.dot_general(
        ones, stacked, (((1,), (1,)), ((), ())), precision=HIGH, preferred_element_type=jnp.float32
    )


def post(message, nvec, sums, cross, square):
    sub = lax.axis_index("sub")
    lane = lax.broadcasted_iota(jnp.int32, (ROWS, message.shape[-1]), 1)
    groups = message.shape[-1] // nvec
    group, place = lane // nvec, lax.rem(lane, nvec)
    pair = jnp.where(place == 0, cross, jnp.where(place == 1, square, 0.0))
    row = jnp.where(group == lax.rem(sub + 1, groups), pair, 0.0)
    row = jnp.where(group == lax.rem(sub, groups), sums, row)
    if len(message.shape) == 3:
        message[...] = jnp.broadcast_to(row[None], message.shape)
    else:
        for at in range(message.shape[0] // ROWS):
            message[at * ROWS : (at + 1) * ROWS, :] = row


def total(x):
    return jnp.sum(x, keepdims=True)


def brought(sources, targets, done):
    copies = [
        pltpu.make_async_copy(source, target, done.at[at])
        for at, (source, target) in enumerate(zip(sources, targets))
    ]
    for copy in copies:
        copy.start()
    return copies


def first_kernel(resid_far, zvec_far, resid, message, zvec, scratch, done):
    for copy in brought((resid_far, zvec_far), (resid, zvec), done):
        copy.wait()
    zero = jnp.zeros((ROWS, message.shape[-1]), jnp.float32)
    post(message, zvec.shape[0], restricted(zvec, resid[...], scratch), zero, zero)


def second_kernel(*refs):
    resid, count = refs[0], (len(refs) - 4) // 2
    sources, targets = refs[1 : 1 + count], refs[1 + count : 1 + 2 * count]
    state, own, done = refs[1 + 2 * count :]
    copies = brought(sources, targets, done)
    copies[0].wait()
    relaxed(targets[0], resid, state)
    block_product(targets[0], state[...], own)
    for copy in copies[1:]:
        copy.wait()


def diag_kernel(vec, dblock, out):
    block_product(dblock, vec[...], out)


def picked(vec, others, cols, part):
    me = lax.axis_index("coarse")
    width = vec.shape[1]
    index = jnp.broadcast_to(cols[pl.ds(part, 1), :], vec.shape)
    owner = index // width
    place = lax.rem(index, width)

    def lanes(block):
        return jnp.take_along_axis(block, place, axis=1, mode="promise_in_bounds")

    if others.shape[0] == 1:
        return jnp.where(owner == me, lanes(vec[...]), lanes(others[0]))
    value = lanes(others[0])
    for at in range(1, others.shape[0]):
        value = jnp.where(owner == at, lanes(others[at]), value)
    return value


def off_rows(lblocks, chosen, start):
    value = rows_times(lblocks.at[0], chosen[0], start)
    for part in range(1, len(chosen)):
        value = value + rows_times(lblocks.at[part], chosen[part], start)
    return value


def sweep_kernel(state, others, own, resid, dblock, lblocks, cols, out, rest):
    chosen = [picked(state, others, cols, part) for part in range(lblocks.shape[0])]

    def body(start):
        here = pl.ds(start, ROWS)
        rest[here, :] = resid[here, :] - (own[here, :] + off_rows(lblocks, chosen, start))

    by_rows(dblock.shape[0], body)
    relaxed(dblock, rest, out, state)


def off_kernel(vec, others, own, lblocks, cols, out):
    chosen = [picked(vec, others, cols, part) for part in range(lblocks.shape[0])]

    def body(start):
        out[pl.ds(start, ROWS), :] = own[pl.ds(start, ROWS), :] + off_rows(lblocks, chosen, start)

    by_rows(out.shape[0], body)


def step_size(arrived, nvec, count):
    lane = lax.broadcasted_iota(jnp.int32, arrived.shape, 1)
    sender = lax.broadcasted_iota(jnp.int32, arrived.shape, 0)
    groups = arrived.shape[1] // nvec
    values = jnp.where(lane // nvec == lax.rem(sender // count + 1, groups), arrived[...], 0.0)
    place = lax.rem(lane, nvec)
    cross = total(jnp.where(place == 0, values, 0.0))
    square = total(jnp.where(place == 1, values, 0.0))
    return cross / (square + 1e-06)


def corrected(state, arrived, inverse, zvec, count):
    nvec, lanes = zvec.shape[0], state.shape[1]
    groups = lanes // nvec
    each = count * groups
    lane = lax.broadcasted_iota(jnp.int32, (each, lanes), 1)
    sender = lax.broadcasted_iota(jnp.int32, (each, lanes), 0)
    keep = lane // nvec == sender // count
    acc = jnp.zeros((nvec, lanes), jnp.float32)
    for at in range(inverse.shape[1] // lanes):
        row = jnp.where(keep, arrived[at * each : (at + 1) * each, :], 0.0)
        acc = acc + inverse[:, at * lanes : (at + 1) * lanes] * jnp.sum(row, axis=0, keepdims=True)
    weights = jnp.broadcast_to(jnp.sum(acc, axis=1, keepdims=True), acc.shape)
    value = state[...]
    for at in range(nvec):
        value = value + weights[at : at + 1, :] * zvec[at].astype(jnp.float32)
    return value


def direction_kernel(count, state, arrived, inverse, zvec, out):
    out[...] = corrected(state, arrived, inverse, zvec, count)


def next_direction_kernel(count, state, arrived, inverse, zvec, previous, resid, image, out, rest, alpha):
    size = step_size(arrived, zvec.shape[0], count)
    out[...] = previous[...] - size * corrected(state, arrived, inverse, zvec, count)
    rest[...] = resid[...] - size * image[...]
    alpha[...] = jnp.broadcast_to(size, alpha.shape)


def near(parts, inner):
    lane = lax.broadcasted_iota(jnp.int32, parts[0].shape, 1)
    value = parts[0][...]
    for at in range(1, len(parts)):
        value = jnp.where(lane < at * inner, value, parts[at][...])
    return value[:, : len(parts) * inner]


def with_interface(known, parts, fblock, out):
    width = fblock.shape[2]
    vec = near(parts, width // len(parts))

    def body(start):
        here = pl.ds(start, ROWS)
        add = rows_times(fblock, vec, start)
        pad = jnp.zeros((ROWS, out.shape[1] - width), jnp.float32)
        out[here, :] = known[here, :] + jnp.concatenate([add, pad], axis=1)

    by_rows(out.shape[0], body)


def image_kernel(known, near0, near1, near2, fblock, resid, dblock, zvec, image, state, own, message, scratch):
    with_interface(known, (near0, near1, near2), fblock, image)
    value = image[...]
    sums = restricted(zvec, value, scratch)
    post(message, zvec.shape[0], sums, total(resid[...] * value), total(value * value))
    relaxed(dblock, image, state)
    block_product(dblock, state[...], own)


def last_image_kernel(nvec, known, near0, near1, near2, fblock, resid, image, message):
    with_interface(known, (near0, near1, near2), fblock, image)
    value = image[...]
    zero = jnp.zeros((ROWS, message.shape[-1]), jnp.float32)
    post(message, nvec, zero, total(resid[...] * value), total(value * value))


def final_kernel(nvec, count, arrived, alpha, first, second, resid, image, field, rest):
    size = step_size(arrived, nvec, count)
    field[0] = alpha[0:1, :] * first[...] + size * second[...]
    rest[0] = resid[...] - size * image[...]


def swap(count, apart):
    return [(low, low ^ apart) for low in range(count) if low ^ apart < count]


def gathered(vec, count):
    if count == 2:
        return lax.ppermute(vec, "coarse", swap(2, 1))[None]
    return lax.all_gather(vec, "coarse", axis=0)


def local(subs, count, right_side, local_blocks, diag_blocks, iface_blocks, block_cols, basis, coarse_inverse):
    shape = right_side.shape[1:]
    nvec = basis.shape[1]
    parcel = (subs * count, shape[1])
    wide = (subs * count, ROWS, shape[1])

    def everywhere(message):
        return lax.all_to_all(message, ("sub", "coarse"), 0, 0, tiled=True)

    def smooth(resid, state, own):
        for sweep in range(SWEEPS - 1):
            others = gathered(state, count)
            if sweep:
                (own,) = call(diag_kernel, [shape], state, dblock, keep=held)
            (state,) = call(
                sweep_kernel, [shape], state, others, own, resid, dblock, lblocks, cols,
                keep=held, scratch=[shape],
            )
        return state

    def apply(vec):
        others = gathered(vec, count)
        near_parts = [lax.ppermute(vec, "sub", swap(subs, 1 << bit)) for bit in range(3)]
        (own,) = call(diag_kernel, [shape], vec, dblock, keep=held)
        (known,) = call(off_kernel, [shape], vec, others, own, lblocks, cols, keep=held)
        return [known, *near_parts, fblock]

    def far(array):
        return pltpu.with_memory_space_constraint(array, pltpu.HBM)

    def near_to(*shapes):
        return [pl.BlockSpec(memory_space=pltpu.VMEM) for _ in shapes]

    zvec, fblock = basis[0], iface_blocks[0]
    outs = [pltpu.VMEM(s, jnp.float32) for s in (shape, wide)]
    resid, message = kernel(
        first_kernel,
        outs,
        [far(right_side[0]), far(zvec)],
        [pltpu.VMEM(zvec.shape, zvec.dtype), (nvec, shape[1]), pltpu.SemaphoreType.DMA((2,))],
        in_specs=[pl.BlockSpec(memory_space=pl.ANY)] * 2,
        out_specs=near_to(*outs),
    )
    arrived = everywhere(message)[:, 0, :]
    sources = [diag_blocks[0], local_blocks[0], block_cols[0], coarse_inverse]
    outs = [pltpu.VMEM(a.shape, a.dtype) for a in sources] + [pltpu.VMEM(shape, jnp.float32)] * 2
    *held, state, own = kernel(
        second_kernel,
        outs,
        [in_vmem(resid), *map(far, sources)],
        [pltpu.SemaphoreType.DMA((len(sources),))],
        in_specs=[pl.BlockSpec(memory_space=pltpu.VMEM)] + [pl.BlockSpec(memory_space=pl.ANY)] * len(sources),
        out_specs=near_to(*outs),
    )
    dblock, lblocks, cols, inverse = held
    held = ()
    state = smooth(resid, state, own)
    (first,) = call(
        functools.partial(direction_kernel, count), [shape], state, arrived, inverse, zvec, keep=held,
    )
    image, state, own, message = call(
        image_kernel, [shape, shape, shape, wide], *apply(first), resid, dblock, zvec,
        keep=held, scratch=[(nvec, shape[1])],
    )
    arrived = everywhere(message)[:, 0, :]
    state = smooth(image, state, own)
    second, rest, alpha = call(
        functools.partial(next_direction_kernel, count), [shape, shape, (ROWS, shape[1])],
        state, arrived, inverse, zvec, first, resid, image, keep=held,
    )
    image, message = call(
        functools.partial(last_image_kernel, nvec), [shape, parcel], *apply(second), rest,
    )
    arrived = everywhere(message)
    operands = [in_vmem(a) for a in (arrived, alpha, first, second, rest, image)]
    return kernel(
        functools.partial(final_kernel, nvec, count),
        [jax.ShapeDtypeStruct((1, *shape), jnp.float32)] * 2,
        operands,
        in_specs=[pl.BlockSpec(memory_space=pltpu.VMEM) for _ in operands],
    )


def solution(mesh):
    placed = (
        P("sub", None, "coarse"),
        P("sub", None, None, None, "coarse"),
        P("sub", None, None, "coarse"),
        P("sub", None, None, "coarse"),
        P("sub", None, "coarse"),
        P("sub", None, None, "coarse"),
        P("sub", None),
    )
    return jax.shard_map(
        functools.partial(local, mesh.shape["sub"], mesh.shape["coarse"]),
        mesh=mesh,
        in_specs=placed,
        out_specs=(P("sub", None, "coarse"), P("sub", None, "coarse")),
        check_vma=False,
    )
```

time: 62.6 us -> 57.4 us (0.917)
  local copies, waits for them, and re-layouts: 8.6 us -> 2.1 us
  waiting for transfers between devices: 9.47 us -> 12 us
  blocking collectives: 11.2 us -> 9.72 us
  Pallas kernels: 13.4 us -> 14.5 us
    unnamed x32 -> x8, local copies, waits for them, and re-layouts: 8.6 us -> 2.08 us
    all_to_all x2, waiting for transfers between devices: 3.47 us -> 5.28 us  [everywhere(): return lax.all_to_all(message, ('sub', 'coarse'), 0, 0, tiled=True)]
    all_to_all x1, blocking collectives: 11.2 us -> 9.72 us  [everywhere(): return lax.all_to_all(message, ('sub', 'coarse'), 0, 0, tiled=True)]
    pallas_call x18 -> x17, Pallas kernels: 13.4 us -> 14.5 us  [kernel(): pl.pallas_call(body, out_shape=outs, scratch_shapes=[pltpu.VMEM(shape, jn...]
    ppermute x6, starting transfers between devices: 5.82 us -> 5 us  [apply(): lax.ppermute(vec, 'sub', swap(subs, 1 << bit))]
  transfers between devices with their start and end apart: 14 -> 14, of which waited for: 10 -> 11; matrix products, arithmetic and copies ran while one was open for 0% -> 0% of each run, Pallas kernels for 15% -> 15%
where the time goes in v2:
time: 57.4 us; the launch traced here: 57 us
  starting transfers between devices  17.9 us (31%)
  Pallas kernels  14.5 us (25%)
  waiting for transfers between devices  12 us (21%)
  blocking collectives  9.72 us (17%)
  local copies, waits for them, and re-layouts  2.1 us (4%)
  between operations  0.82 us (1%)
    pallas_call x17, Pallas kernels, kernel(): pl.pallas_call(body, out_shape=outs, scratch_shapes=[pltpu.VMEM(shape, jn...  14.5 us
    all_to_all x2, starting transfers between devices, everywhere(): return lax.all_to_all(message, ('sub', 'coarse'), 0, 0, tiled=True)  11 us
    all_to_all x1, blocking collectives, everywhere(): return lax.all_to_all(message, ('sub', 'coarse'), 0, 0, tiled=True)  9.72 us
    all_to_all x2, waiting for transfers between devices, everywhere(): return lax.all_to_all(message, ('sub', 'coarse'), 0, 0, tiled=True)  5.28 us
    ppermute x6, starting transfers between devices, apply(): lax.ppermute(vec, 'sub', swap(subs, 1 << bit))  5 us
    ppermute x6, waiting for transfers between devices, apply(): lax.ppermute(vec, 'sub', swap(subs, 1 << bit))  3.52 us
    ppermute x6, waiting for transfers between devices, gathered(): return lax.ppermute(vec, 'coarse', swap(2, 1))[None]  3.21 us
    unnamed x8, local copies, waits for them, and re-layouts  2.08 us
  transfers between devices with their start and end apart: 14, of which 11 were waited for; matrix products, arithmetic and copies ran while one was open for 0% of the time, Pallas kernels for 15%

profile of v2, /device:TPU:0, one launch (start us, length us, event | category | flops | bytes accessed | tf_op | source)
XLA Modules:
  0.0 57.0 jit_solution(14218980103918857692)
XLA Ops:
  0.6 2.1 %shard_map.86 = (f32[64,128]{1,0:T(8,128)S(1)}, f32[32,8,128]{2,1,0:T(8,128)}) custom-call(f32[64,128]{1,0:T(8,128)} %bitcast.40, bf16[32,64,128]{2,1,0:T(8,128)(2,1)} %bitcast.22), custom_call_target="tpu_custom_call" | custom-call | tf_op jit(solution)/shard_map/pallas_call | solution.py:22
  2.8 7.3 %all-to-all-start = ((f32[32,8,128]{2,1,0:T(8,128)}), f32[32,8,128]{2,1,0:T(8,128)S(1)}, u32[]{:S(2)}, u32[]{:S(2)}) async-start(f32[32,8,128]{2,1,0:T(8,128)} %get-tuple-element.25), calls=%async_computation | async-start | bytes 262144 | tf_op jit(solution)/shard_map/all_to_all | solution.py:290
  10.1 2.0 %shard_map.87 = (bf16[64,64,128]{2,1,0:T(8,128)(2,1)S(1)}, bf16[2,64,64,128]{3,2,1,0:T(8,128)(2,1)S(1)}, s32[2,128]{1,0:T(2,128)S(1)}, f32[32,512]{1,0:T(8,128)S...) custom-call(f32[64,128]{1,0:T(8,128)S(1)} %get-tuple-element.19.refs_0_.refs_3_.refs_5_, ...), custom_call_target="tpu_custom_call" | custom-call | tf_op jit(solution)/shard_map/pallas_call | solution.py:22
  12.0 0.3 collective-permute-start
  12.4 1.0 %collective-permute-done = f32[64,128]{1,0:T(8,128)S(1)} collective-permute-done((f32[64,128]{1,0:T(8,128)S(1)}, f32[64,128]{1,0:T(8,128)S(1)}, u32[]{:S(2)}, u32[]{:S(2)}) %collective-permute-start) | collective-permute-done | bytes 32800 | tf_op jit(solution)/shard_map/ppermute | solution.py:279
  13.3 1.0 %shard_map.88.refs_0_ = f32[64,128]{1,0:T(8,128)S(1)} custom-call(f32[64,128]{1,0:T(8,128)S(1)} %get-tuple-element.20.refs_0_, f32[1,64,128]{2,1,0:T(8,128)S(1)} %bitcast.34, f32[64,128]{1,0:T(8,128)S(1)} %get-tuple-element.21.refs_2_, f32[64,128]{1,0:T(8,128)S(1)} %get-tuple-element.19.refs_0_.refs_3_.refs_5_, ...), custom_call_target="tpu_custom_call" | custom-call | tf_op jit(solution)/shard_map/pallas_call | solution.py:22
  14.3 0.3 collective-permute-start.1
  14.7 0.3 shard_map.89.refs_2_
  15.0 0.6 %collective-permute-done.1 = f32[64,128]{1,0:T(8,128)S(1)} collective-permute-done((f32[64,128]{1,0:T(8,128)S(1)}, f32[64,128]{1,0:T(8,128)S(1)}, u32[]{:S(2)}, u32[]{:S(2)}) %collective-permute-start.1) | collective-permute-done | bytes 32800 | tf_op jit(solution)/shard_map/ppermute | solution.py:279
  15.6 1.0 %shard_map.90.refs_0_ = f32[64,128]{1,0:T(8,128)S(1)} custom-call(f32[64,128]{1,0:T(8,128)S(1)} %shard_map.88.refs_0_, f32[1,64,128]{2,1,0:T(8,128)S(1)} %bitcast.35, f32[64,128]{1,0:T(8,128)S(1)} %shard_map.89.refs_2_, f32[64,128]{1,0:T(8,128)S(1)} %get-tuple-element.19.refs_0_.refs_3_.refs_5_, ...), custom_call_target="tpu_custom_call" | custom-call | tf_op jit(solution)/shard_map/pallas_call | solution.py:22
  16.6 1.7 %all-to-all-done = f32[32,8,128]{2,1,0:T(8,128)S(1)} async-done(((f32[32,8,128]{2,1,0:T(8,128)}), f32[32,8,128]{2,1,0:T(8,128)S(1)}, u32[]{:S(2)}, u32[]{:S(2)}) %all-to-all-start) | async-done | bytes 131104 | tf_op jit(solution)/shard_map/all_to_all | solution.py:290
  18.3 0.0 copy-start
  18.3 1.0 %copy-done = bf16[1,32,64,128]{3,2,1,0:T(8,128)(2,1)S(1)} copy-done((bf16[1,32,64,128]{3,2,1,0:T(8,128)(2,1)S(1)}, bf16[1,32,64,128]{3,2,1,0:T(8,128)(2,1)}, u32[]{:S(2)}) %copy-start) | copy-done | bytes 524312
  19.4 0.2 shard_map.91.refs_0_.refs_4_.first
  19.6 0.3 collective-permute-start.2
  19.8 0.4 collective-permute-start.3
  20.2 1.2 %collective-permute-start.4 = (f32[64,128]{1,0:T(8,128)S(1)}, f32[64,128]{1,0:T(8,128)S(1)}, u32[]{:S(2)}, u32[]{:S(2)}) collective-permute-start(f32[64,128]{1,0:T(8,128)S(1)} %shard_map.91.refs_0_.refs_4_.first), channel_id=1, source_target_pairs={{0,4},{2,6},{4,0},{6,2},{8,12},{10,14},{12,8},{14,10},{16,20},{18,... | collective-permute-start | bytes 98312 | tf_op jit(solution)/shard_map/ppermute | solution.py:305
  21.4 1.5 %collective-permute-start.5 = (f32[64,128]{1,0:T(8,128)S(1)}, f32[64,128]{1,0:T(8,128)S(1)}, u32[]{:S(2)}, u32[]{:S(2)}) collective-permute-start(f32[64,128]{1,0:T(8,128)S(1)} %shard_map.91.refs_0_.refs_4_.first), channel_id=1, source_target_pairs={{0,8},{2,10},{4,12},{6,14},{8,0},{10,2},{12,4},{14,6},{16,24},{18,... | collective-permute-start | bytes 98312 | tf_op jit(solution)/shard_map/ppermute | solution.py:305
  22.8 0.3 shard_map.92.refs_2_
  23.2 0.0 collective-permute-done.2
  23.2 0.7 %shard_map.93.refs_0_ = f32[64,128]{1,0:T(8,128)S(1)} custom-call(f32[64,128]{1,0:T(8,128)S(1)} %shard_map.91.refs_0_.refs_4_.first, f32[1,64,128]{2,1,0:T(8,128)S(1)} %bitcast.32, f32[64,128]{1,0:T(8,128)S(1)} %shard_map.92.refs_2_, bf16[2,64,64,128]{3,2,1,0:T(8,128)(2,1)S(1)} %get-tuple-element.23.refs_5_.refs_3_, ...), custom_call_target="tpu_custom_call" | custom-call | tf_op jit(solution)/shard_map/pallas_call | solution.py:22
  23.9 0.3 collective-permute-done.4.refs_2_
  24.1 1.2 %collective-permute-done.5.refs_3_ = f32[64,128]{1,0:T(8,128)S(1)} collective-permute-done((f32[64,128]{1,0:T(8,128)S(1)}, f32[64,128]{1,0:T(8,128)S(1)}, u32[]{:S(2)}, u32[]{:S(2)}) %collective-permute-start.5) | collective-permute-done | bytes 32800 | tf_op jit(solution)/shard_map/ppermute | solution.py:305
  25.3 2.0 %shard_map.94 = (f32[64,128]{1,0:T(8,128)S(1)}, f32[64,128]{1,0:T(8,128)S(1)}, f32[64,128]{1,0:T(8,128)S(1)}, f32[32,8,128]{2,1,0:T(8,128)}) custom-call(f32[64,128]{1,0:T(8,128)S(1)} %shard_map.93.refs_0_, f32[64,128]{1,0:T(8,128)S(1)} %collective-permute-done.3.refs_1_, f32[64,128]{1,0:T(8,128)S(1)} %collective-permute-done.4.refs_2_, ...), custom_call_target="tpu_custom_call" | custom-call | tf_op jit(solution)/shard_map/pallas_call | solution.py:22
  27.3 3.7 %all-to-all-start.1 = ((f32[32,8,128]{2,1,0:T(8,128)}), f32[32,8,128]{2,1,0:T(8,128)S(1)}, u32[]{:S(2)}, u32[]{:S(2)}) async-start(f32[32,8,128]{2,1,0:T(8,128)} %get-tuple-element.30), calls=%async_computation.1 | async-start | bytes 262144 | tf_op jit(solution)/shard_map/all_to_all | solution.py:290
  31.1 0.3 collective-permute-start.6
  31.4 1.0 %collective-permute-done.6 = f32[64,128]{1,0:T(8,128)S(1)} collective-permute-done((f32[64,128]{1,0:T(8,128)S(1)}, f32[64,128]{1,0:T(8,128)S(1)}, u32[]{:S(2)}, u32[]{:S(2)}) %collective-permute-start.6) | collective-permute-done | bytes 32800 | tf_op jit(solution)/shard_map/ppermute | solution.py:279
  32.3 1.0 %shard_map.95.refs_0_ = f32[64,128]{1,0:T(8,128)S(1)} custom-call(f32[64,128]{1,0:T(8,128)S(1)} %get-tuple-element.27.refs_0_, f32[1,64,128]{2,1,0:T(8,128)S(1)} %bitcast.33, f32[64,128]{1,0:T(8,128)S(1)} %get-tuple-element.28.refs_2_, f32[64,128]{1,0:T(8,128)S(1)} %get-tuple-element.29.refs_3_.refs_6_, ...), custom_call_target="tpu_custom_call" | custom-call | tf_op jit(solution)/shard_map/pallas_call | solution.py:22
  33.4 0.3 collective-permute-start.7
  33.7 0.3 shard_map.96.refs_2_
  34.0 0.6 %collective-permute-done.7 = f32[64,128]{1,0:T(8,128)S(1)} collective-permute-done((f32[64,128]{1,0:T(8,128)S(1)}, f32[64,128]{1,0:T(8,128)S(1)}, u32[]{:S(2)}, u32[]{:S(2)}) %collective-permute-start.7) | collective-permute-done | bytes 32800 | tf_op jit(solution)/shard_map/ppermute | solution.py:279
  34.6 1.0 %shard_map.97.refs_0_ = f32[64,128]{1,0:T(8,128)S(1)} custom-call(f32[64,128]{1,0:T(8,128)S(1)} %shard_map.95.refs_0_, f32[1,64,128]{2,1,0:T(8,128)S(1)} %bitcast.36, f32[64,128]{1,0:T(8,128)S(1)} %shard_map.96.refs_2_, f32[64,128]{1,0:T(8,128)S(1)} %get-tuple-element.29.refs_3_.refs_6_, bf16[64,64,128]{2,1,0:T(8,128)(2,1)S(1)} %get-tuple-element.22.refs_4_.refs_1_.refs_6_, ...), custom_call_target="tpu_custom_call" | custom-call | tf_op jit(solution)/shard_map/pallas_call | solution.py:22
  35.7 3.6 %all-to-all-done.1 = f32[32,8,128]{2,1,0:T(8,128)S(1)} async-done(((f32[32,8,128]{2,1,0:T(8,128)}), f32[32,8,128]{2,1,0:T(8,128)S(1)}, u32[]{:S(2)}, u32[]{:S(2)}) %all-to-all-start.1) | async-done | bytes 131104 | tf_op jit(solution)/shard_map/all_to_all | solution.py:290
  39.3 0.0 copy-start.1
  39.3 1.0 %copy-done.1 = bf16[1,32,64,128]{3,2,1,0:T(8,128)(2,1)S(1)} copy-done((bf16[1,32,64,128]{3,2,1,0:T(8,128)(2,1)S(1)}, bf16[1,32,64,128]{3,2,1,0:T(8,128)(2,1)}, u32[]{:S(2)}) %copy-start.1) | copy-done | bytes 524312
  40.4 0.2 shard_map.98
  40.6 0.3 collective-permute-start.8
  40.9 0.5 collective-permute-start.10
  41.4 0.7 %collective-permute-start.11 = (f32[64,128]{1,0:T(8,128)S(1)}, f32[64,128]{1,0:T(8,128)S(1)}, u32[]{:S(2)}, u32[]{:S(2)}) collective-permute-start(f32[64,128]{1,0:T(8,128)S(1)} %get-tuple-element.31.refs_0_.second), channel_id=1, source_target_pairs={{0,8},{2,10},{4,12},{6,14},{8,0},{10,2},{12,4},{14,6},{16,24},{18,... | collective-permute-start | bytes 98312 | tf_op jit(solution)/shard_map/ppermute | solution.py:305
  42.0 0.8 %collective-permute-start.9 = (f32[64,128]{1,0:T(8,128)S(1)}, f32[64,128]{1,0:T(8,128)S(1)}, u32[]{:S(2)}, u32[]{:S(2)}) collective-permute-start(f32[64,128]{1,0:T(8,128)S(1)} %get-tuple-element.31.refs_0_.second), channel_id=1, source_target_pairs={{0,2},{2,0},{4,6},{6,4},{8,10},{10,8},{12,14},{14,12},{16,18},{18,... | collective-permute-start | bytes 98312 | tf_op jit(solution)/shard_map/ppermute | solution.py:305
  42.8 0.3 shard_map.99.refs_2_
  43.2 0.7 %shard_map.100.refs_0_ = f32[64,128]{1,0:T(8,128)S(1)} custom-call(f32[64,128]{1,0:T(8,128)S(1)} %get-tuple-element.31.refs_0_.second, f32[1,64,128]{2,1,0:T(8,128)S(1)} %bitcast.31, f32[64,128]{1,0:T(8,128)S(1)} %shard_map.99.refs_2_, bf16[2,64,64,128]{3,2,1,0:T(8,128)(2,1)S(1)} %get-tuple-element.23.refs_5_.refs_3_, ...), custom_call_target="tpu_custom_call" | custom-call | tf_op jit(solution)/shard_map/pallas_call | solution.py:22
  43.9 0.9 %collective-permute-done.10.refs_2_ = f32[64,128]{1,0:T(8,128)S(1)} collective-permute-done((f32[64,128]{1,0:T(8,128)S(1)}, f32[64,128]{1,0:T(8,128)S(1)}, u32[]{:S(2)}, u32[]{:S(2)}) %collective-permute-start.10) | collective-permute-done | bytes 32800 | tf_op jit(solution)/shard_map/ppermute | solution.py:305
  44.8 0.5 collective-permute-done.11.refs_3_
  45.3 0.7 %collective-permute-done.9.refs_1_ = f32[64,128]{1,0:T(8,128)S(1)} collective-permute-done((f32[64,128]{1,0:T(8,128)S(1)}, f32[64,128]{1,0:T(8,128)S(1)}, u32[]{:S(2)}, u32[]{:S(2)}) %collective-permute-start.9) | collective-permute-done | bytes 32800 | tf_op jit(solution)/shard_map/ppermute | solution.py:305
  45.9 0.6 shard_map.101
  46.5 9.7 %all_to_all.21 = f32[32,1,128]{2,1,0:T(1,128)S(1)} all-to-all(f32[32,1,128]{2,1,0:T(1,128)S(1)} %bitcast.37), channel_id=1, replica_groups=mesh['sub'=16,'coarse'=2] {'sub','coarse'}, dimensions={0} | all-to-all | bytes 32768 | tf_op jit(solution)/shard_map/all_to_all | solution.py:290
  56.2 0.8 %shard_map.102 = (f32[1,64,128]{2,1,0:T(8,128)}, f32[1,64,128]{2,1,0:T(8,128)}) custom-call(f32[32,128]{1,0:T(8,128)S(1)} %bitcast.28, f32[8,128]{1,0:T(8,128)S(1)} %get-tuple-element.34.alpha, f32[64,128]{1,0:T(8,128)S(1)} %shard_map.91.refs_0_.refs_4_.first, f32[64,128]{1,0:T(8,128)S(1)} %get-tuple-element.31.refs_0_.second, ...), custom_call_target="tpu_custom_call" | custom-call | tf_op jit(solution)/shard_map/pallas_call | solution.py:22
  (8 shorter events, 0.0 us)
Async XLA Ops:
  2.8 15.5 %all-to-all-start = ((f32[32,8,128]{2,1,0:T(8,128)}), f32[32,8,128]{2,1,0:T(8,128)S(1)}, u32[]{:S(2)}, u32[]{:S(2)}) async-start(f32[32,8,128]{2,1,0:T(8,128)} %get-tuple-element.25), calls=%async_computation | async-start | bytes 262144 | tf_op jit(solution)/shard_map/all_to_all | solution.py:290
  12.0 1.3 %collective-permute-start = (f32[64,128]{1,0:T(8,128)S(1)}, f32[64,128]{1,0:T(8,128)S(1)}, u32[]{:S(2)}, u32[]{:S(2)}) collective-permute-start(f32[64,128]{1,0:T(8,128)S(1)} %get-tuple-element.20.refs_0_), channel_id=1, source_target_pairs={{0,1},{1,0},{2,3},{3,2},{4,5},{5,4},{6,7},{7,6},{8,9},{9,8},{10,11... | collective-permute-start | bytes 98312 | tf_op jit(solution)/shard_map/ppermute | solution.py:279
  14.3 1.3 %collective-permute-start.1 = (f32[64,128]{1,0:T(8,128)S(1)}, f32[64,128]{1,0:T(8,128)S(1)}, u32[]{:S(2)}, u32[]{:S(2)}) collective-permute-start(f32[64,128]{1,0:T(8,128)S(1)} %shard_map.88.refs_0_), channel_id=1, source_target_pairs={{0,1},{1,0},{2,3},{3,2},{4,5},{5,4},{6,7},{7,6},{8,9},{9,8},{10,11... | collective-permute-start | bytes 98312 | tf_op jit(solution)/shard_map/ppermute | solution.py:279
  18.3 1.0 %copy-start = (bf16[1,32,64,128]{3,2,1,0:T(8,128)(2,1)S(1)}, bf16[1,32,64,128]{3,2,1,0:T(8,128)(2,1)}, u32[]{:S(2)}) copy-start(bf16[1,32,64,128]{3,2,1,0:T(8,128)(2,1)} %param.12) | copy-start | bytes 1572868
  19.4 5.9 %copy-start.2 = (bf16[1,64,64,96]{3,2,1,0:T(8,128)(2,1)S(1)}, bf16[1,64,64,96]{3,2,1,0:T(8,128)(2,1)}, u32[]{:S(2)}) copy-start(bf16[1,64,64,96]{3,2,1,0:T(8,128)(2,1)} %param.10) | copy-start | bytes 2359300
  19.6 3.6 %collective-permute-start.2 = (f32[64,128]{1,0:T(8,128)S(1)}, f32[64,128]{1,0:T(8,128)S(1)}, u32[]{:S(2)}, u32[]{:S(2)}) collective-permute-start(f32[64,128]{1,0:T(8,128)S(1)} %shard_map.91.refs_0_.refs_4_.first), channel_id=1, source_target_pairs={{0,1},{1,0},{2,3},{3,2},{4,5},{5,4},{6,7},{7,6},{8,9},{9,8},{10,11... | collective-permute-start | bytes 98312 | tf_op jit(solution)/shard_map/ppermute | solution.py:279
  19.8 4.0 %collective-permute-start.3 = (f32[64,128]{1,0:T(8,128)S(1)}, f32[64,128]{1,0:T(8,128)S(1)}, u32[]{:S(2)}, u32[]{:S(2)}) collective-permute-start(f32[64,128]{1,0:T(8,128)S(1)} %shard_map.91.refs_0_.refs_4_.first), channel_id=1, source_target_pairs={{0,2},{2,0},{4,6},{6,4},{8,10},{10,8},{12,14},{14,12},{16,18},{18,... | collective-permute-start | bytes 98312 | tf_op jit(solution)/shard_map/ppermute | solution.py:305
  20.2 3.9 %collective-permute-start.4 = (f32[64,128]{1,0:T(8,128)S(1)}, f32[64,128]{1,0:T(8,128)S(1)}, u32[]{:S(2)}, u32[]{:S(2)}) collective-permute-start(f32[64,128]{1,0:T(8,128)S(1)} %shard_map.91.refs_0_.refs_4_.first), channel_id=1, source_target_pairs={{0,4},{2,6},{4,0},{6,2},{8,12},{10,14},{12,8},{14,10},{16,20},{18,... | collective-permute-start | bytes 98312 | tf_op jit(solution)/shard_map/ppermute | solution.py:305
  21.4 3.9 %collective-permute-start.5 = (f32[64,128]{1,0:T(8,128)S(1)}, f32[64,128]{1,0:T(8,128)S(1)}, u32[]{:S(2)}, u32[]{:S(2)}) collective-permute-start(f32[64,128]{1,0:T(8,128)S(1)} %shard_map.91.refs_0_.refs_4_.first), channel_id=1, source_target_pairs={{0,8},{2,10},{4,12},{6,14},{8,0},{10,2},{12,4},{14,6},{16,24},{18,... | collective-permute-start | bytes 98312 | tf_op jit(solution)/shard_map/ppermute | solution.py:305
  27.3 12.0 %all-to-all-start.1 = ((f32[32,8,128]{2,1,0:T(8,128)}), f32[32,8,128]{2,1,0:T(8,128)S(1)}, u32[]{:S(2)}, u32[]{:S(2)}) async-start(f32[32,8,128]{2,1,0:T(8,128)} %get-tuple-element.30), calls=%async_computation.1 | async-start | bytes 262144 | tf_op jit(solution)/shard_map/all_to_all | solution.py:290
  31.1 1.3 %collective-permute-start.6 = (f32[64,128]{1,0:T(8,128)S(1)}, f32[64,128]{1,0:T(8,128)S(1)}, u32[]{:S(2)}, u32[]{:S(2)}) collective-permute-start(f32[64,128]{1,0:T(8,128)S(1)} %get-tuple-element.27.refs_0_), channel_id=1, source_target_pairs={{0,1},{1,0},{2,3},{3,2},{4,5},{5,4},{6,7},{7,6},{8,9},{9,8},{10,11... | collective-permute-start | bytes 98312 | tf_op jit(solution)/shard_map/ppermute | solution.py:279
  33.4 1.3 %collective-permute-start.7 = (f32[64,128]{1,0:T(8,128)S(1)}, f32[64,128]{1,0:T(8,128)S(1)}, u32[]{:S(2)}, u32[]{:S(2)}) collective-permute-start(f32[64,128]{1,0:T(8,128)S(1)} %shard_map.95.refs_0_), channel_id=1, source_target_pairs={{0,1},{1,0},{2,3},{3,2},{4,5},{5,4},{6,7},{7,6},{8,9},{9,8},{10,11... | collective-permute-start | bytes 98312 | tf_op jit(solution)/shard_map/ppermute | solution.py:279
  39.3 1.0 %copy-start.1 = (bf16[1,32,64,128]{3,2,1,0:T(8,128)(2,1)S(1)}, bf16[1,32,64,128]{3,2,1,0:T(8,128)(2,1)}, u32[]{:S(2)}) copy-start(bf16[1,32,64,128]{3,2,1,0:T(8,128)(2,1)} %param.12) | copy-start | bytes 1572868
  40.3 5.6 %copy-start.3 = (bf16[1,64,64,96]{3,2,1,0:T(8,128)(2,1)S(1)}, bf16[1,64,64,96]{3,2,1,0:T(8,128)(2,1)}, u32[]{:S(2)}) copy-start(bf16[1,64,64,96]{3,2,1,0:T(8,128)(2,1)} %param.10) | copy-start | bytes 2359300
  40.6 2.6 %collective-permute-start.8 = (f32[64,128]{1,0:T(8,128)S(1)}, f32[64,128]{1,0:T(8,128)S(1)}, u32[]{:S(2)}, u32[]{:S(2)}) collective-permute-start(f32[64,128]{1,0:T(8,128)S(1)} %get-tuple-element.31.refs_0_.second), channel_id=1, source_target_pairs={{0,1},{1,0},{2,3},{3,2},{4,5},{5,4},{6,7},{7,6},{8,9},{9,8},{10,11... | collective-permute-start | bytes 98312 | tf_op jit(solution)/shard_map/ppermute | solution.py:279
  40.9 3.9 %collective-permute-start.10 = (f32[64,128]{1,0:T(8,128)S(1)}, f32[64,128]{1,0:T(8,128)S(1)}, u32[]{:S(2)}, u32[]{:S(2)}) collective-permute-start(f32[64,128]{1,0:T(8,128)S(1)} %get-tuple-element.31.refs_0_.second), channel_id=1, source_target_pairs={{0,4},{2,6},{4,0},{6,2},{8,12},{10,14},{12,8},{14,10},{16,20},{18,... | collective-permute-start | bytes 98312 | tf_op jit(solution)/shard_map/ppermute | solution.py:305
  41.4 3.9 %collective-permute-start.11 = (f32[64,128]{1,0:T(8,128)S(1)}, f32[64,128]{1,0:T(8,128)S(1)}, u32[]{:S(2)}, u32[]{:S(2)}) collective-permute-start(f32[64,128]{1,0:T(8,128)S(1)} %get-tuple-element.31.refs_0_.second), channel_id=1, source_target_pairs={{0,8},{2,10},{4,12},{6,14},{8,0},{10,2},{12,4},{14,6},{16,24},{18,... | collective-permute-start | bytes 98312 | tf_op jit(solution)/shard_map/ppermute | solution.py:305
  42.0 3.9 %collective-permute-start.9 = (f32[64,128]{1,0:T(8,128)S(1)}, f32[64,128]{1,0:T(8,128)S(1)}, u32[]{:S(2)}, u32[]{:S(2)}) collective-permute-start(f32[64,128]{1,0:T(8,128)S(1)} %get-tuple-element.31.refs_0_.second), channel_id=1, source_target_pairs={{0,2},{2,0},{4,6},{6,4},{8,10},{10,8},{12,14},{14,12},{16,18},{18,... | collective-permute-start | bytes 98312 | tf_op jit(solution)/shard_map/ppermute | solution.py:305
